TPU v7x, 32 devices: a whole 2x2x4 slice. The times are simulated.
32 devices in a mesh: grp: 2 (over y), side: 4 (over z), shard: 4 (over x, core).
Axes of the slice: x: 2, y: 2, z: 4, core: 2. Of those that a mesh axis runs over, the one named last changes fastest.
Arguments:
- queries: bfloat16 [480, 8192], P(('grp', 'side', 'shard')), parts along dimension 0, may hold values from -6.5 to 6.5
- new_kv: bfloat16 [480, 2048], P(('grp', 'side', 'shard')), parts along dimension 0, may hold values from -4.5 to 4.5
- kv_pool: bfloat16 [3584, 16, 2048], P(('grp', 'side', 'shard')), parts along dimension 0, may hold values from -4.5 to 4.5
- page_table: int32 [480, 16], P(('grp', 'side', 'shard')), parts along dimension 0, may hold values from 0 to 111, as said below
- ctx_len: int32 [480], P(('grp', 'side', 'shard')), parts along dimension 0, may hold values from 0 to 256, as said below
- residual_in: bfloat16 [480, 8192], P(('grp', 'side', 'shard')), parts along dimension 0, may hold values from -6 to 6
- norm_gain: bfloat16 [8192], replicated, may hold values from 0.5 to 1.5
- w_up: bfloat16 [8192, 16384], P('side', 'shard'), may hold values from -0.0625 to 0.0625
- w_down: bfloat16 [16384, 8192], P('shard', 'side'), may hold values from -0.046875 to 0.046875
Outputs:
- layer_out: bfloat16 [480, 8192], P(('grp', 'side', 'shard')), parts along dimension 0
There are 2 independent parts, one for each index of `grp`. A program takes and returns all parts, laid end to end along the dimension named above; an argument that names none is the same for every part. Nothing has to cross between parts.
Inputs may be any that keep to these rules, and one draw needn't show every extreme that they name: `ctx_len`: on one device's 15 slots, 3 to 12 have a nonzero length, exactly 12 on some device; a live slot's pages together hold at most 112 pages on its device; every device has a slot of length 256. `page_table`: the first ceil(ctx_len / 16) entries of a live slot name distinct pages, and no page is named by two live slots of one device; other entries name valid pages.
All inputs are finite; a program needn't handle non-finite values.
Results may differ from a plain program's by a relative error of at most 0.009.
Values may be sent and summed in bfloat16 or wider, within the bound.
No kernel may reach another device: no remote copies, remote signals or barrier semaphores. Data moves between devices by JAX's collectives and lax.ppermute only.
A program may use at most 128 MiB of HBM per device.

v0:
```python
import functools
import math

import jax
import jax.numpy as jnp
from jax import lax
from jax.experimental import pallas as pl
from jax.experimental.pallas import tpu as pltpu
from jax.sharding import PartitionSpec as P

KV_HEADS = 8
HEAD = 128
GROUP = 8
LIVE_CAP = 12
PAD = 16

epsilon = 1e-05
bf16, f32, i32 = jnp.bfloat16, jnp.float32, jnp.int32
VMEM_MB = 1 << 20


def params(mb, **more):
    return pltpu.CompilerParams(vmem_limit_bytes=mb * VMEM_MB, **more)


def cost(flops, bytes_accessed):
    return pl.CostEstimate(
        flops=int(flops) // 64, bytes_accessed=int(bytes_accessed) // 64, transcendentals=0
    )


def pad_rows(x):
    rows = x.shape[0]
    if rows == PAD:
        return x
    return jnp.concatenate([x, jnp.zeros((PAD - rows,) + x.shape[1:], x.dtype)], axis=0)


def live_ranks(lengths, slots):
    live, rank, count = [], [], jnp.int32(0)
    for slot in range(slots):
        alive = lengths[slot] > 0
        live.append(alive)
        rank.append(count)
        count = count + alive.astype(i32)
    return live, rank


def token_bias(lengths, table, pages, page):
    slots, entries = table.shape
    tokens = pages * page
    lanes = 128 * ((pages + 127) // 128)
    row = lax.broadcasted_iota(i32, (PAD, lanes), 0)
    column = lax.broadcasted_iota(i32, (PAD, lanes), 1)
    reach = jnp.zeros((PAD, lanes), i32)
    for slot in range(slots):
        reach = jnp.where(row == slot, lengths[slot], reach)
    table = pad_rows(table)
    seen = jnp.zeros((PAD, lanes), i32)
    for entry in range(entries):
        here = jnp.minimum(jnp.maximum(reach - entry * page, 0), page)
        seen = seen + jnp.where(table[:, entry : entry + 1] == column, here, 0)
    spread = (
        lax.broadcasted_iota(i32, (lanes, tokens), 1) // page
        == lax.broadcasted_iota(i32, (lanes, tokens), 0)
    )
    seen_tokens = jnp.dot(
        seen.astype(f32).astype(bf16), spread.astype(f32).astype(bf16), preferred_element_type=f32
    )
    place = (lax.broadcasted_iota(i32, (PAD, tokens), 1) % page).astype(f32)
    return jnp.where(place < seen_tokens, 0.0, -1e30)


def live_pick(lengths, slots, rows, offset, to_slots):
    live, rank = live_ranks(lengths, slots)
    shape = (PAD, rows) if to_slots else (rows, PAD)
    of_slot = lax.broadcasted_iota(i32, shape, 0 if to_slots else 1)
    of_rank = lax.broadcasted_iota(i32, shape, 1 if to_slots else 0) - offset
    pick = jnp.zeros(shape, f32)
    for slot in range(slots):
        chosen = jnp.logical_and(of_rank == rank[slot], of_slot == slot)
        pick = jnp.where(jnp.logical_and(chosen, live[slot]), 1.0, pick)
    return pick.astype(bf16), rank[-1] + live[-1].astype(i32)


POOL_CUTS = 4


def attend_kernel(lengths, side, *refs, masks, sides, first):
    refs = list(refs)
    take = lambda n: [refs.pop(0) for _ in range(n)]
    if first:
        table_ref = refs.pop(0)
        sources = take(4)
    else:
        q_ref, new_ref, res_ref, gain_ref, bias_ref = take(5)
    pool_source = refs.pop(0)
    sends, mixed_refs = take(len(masks)), take(len(masks))
    square_ref = refs.pop(0)
    if first:
        q_ref, new_ref, res_ref, gain_ref, bias_ref, gain_copy, sems = take(7)
    pool_ref, pool_sems = refs
    slots, step = mixed_refs[0].shape
    pages, page, width = pool_source.shape
    columns = width // 2 // sides
    heads = columns // HEAD
    tokens = pages * page
    scale = math.log2(math.e) / math.sqrt(HEAD)

    if first:
        small = [
            pltpu.make_async_copy(source, target, sems.at[n])
            for n, (source, target) in enumerate(
                zip(sources, (q_ref, new_ref, res_ref, gain_copy), strict=True)
            )
        ]
        for copy in small:
            copy.start()
    cut, half, pair = pages // POOL_CUTS, width // 2, columns * 2
    here = ((side[0] ^ masks[0]) // 2) * pair
    brought = []
    for n, at in enumerate((here, half + here)):
        columns_at = pl.ds(pl.multiple_of(at, pair), pair)
        target_at = pl.ds(n * pair, pair)
        brought.append([])
        for c in range(POOL_CUTS):
            rows = pl.ds(c * cut, cut)
            copy = pltpu.make_async_copy(
                pool_source.at[rows, :, columns_at], pool_ref.at[rows, :, target_at], pool_sems.at[n, c]
            )
            copy.start()
            brought[n].append(copy)
    if first:
        bias_ref[...] = token_bias(lengths, table_ref[...], pages, page)
        for copy in small:
            copy.wait()
        gain_ref[...] = gain_copy[...].astype(f32)
    for copy in brought[0]:
        copy.wait()
    values_to_come = brought[1]

    pick, count = live_pick(lengths, slots, PAD, 0, False)
    squares = jnp.zeros((slots, HEAD), f32)
    bias = bias_ref[...][None]
    jobs = [(n, head) for n in range(len(masks)) for head in range(heads)]

    def places(job):
        block, base = side[0] ^ masks[job[0]], job[1] * GROUP * HEAD
        new_at = pl.multiple_of(block * columns, columns) + job[1] * HEAD
        key_at = pl.multiple_of(lax.rem(block, 2) * columns, columns) + job[1] * HEAD
        return block, base, pl.multiple_of(block * step, step) + base, new_at, key_at

    def score(job):
        _, _, start, new_at, key_at = places(job)
        q = jnp.concatenate(
            [pad_rows(q_ref[:, pl.ds(start + g * HEAD, HEAD)]) for g in range(GROUP)], axis=0
        )
        keys = pool_ref[:, :, pl.ds(key_at, HEAD)].reshape(tokens, HEAD)
        new_key = pad_rows(new_ref[:, pl.ds(new_at, HEAD)]).astype(f32)
        scores = lax.dot_general(q, keys, (((1,), (1,)), ((), ())), preferred_element_type=f32)
        own = jnp.sum(
            q.astype(f32).reshape(GROUP, PAD, HEAD) * new_key[None], axis=-1, keepdims=True
        )
        return scores.reshape(GROUP, PAD, tokens), own * scale

    ready = score(jobs[0])
    for number, job in enumerate(jobs):
        block, base, start, new_at, key_at = places(job)
        scores, own = ready
        if number + 1 < len(jobs):
            ready = score(jobs[number + 1])
        scores = scores * scale + bias
        highest = jnp.maximum(jnp.max(scores, axis=-1, keepdims=True), own)
        weights = jnp.exp2(scores - highest)
        own_weight = jnp.exp2(own - highest)
        total = jnp.sum(weights, axis=-1, keepdims=True) + own_weight
        for copy in values_to_come:
            copy.wait()
        values_to_come = []
        values = pool_ref[:, :, pl.ds(pair + key_at, HEAD)].reshape(tokens, HEAD)
        new_value = pad_rows(new_ref[:, pl.ds(half + new_at, HEAD)]).astype(f32)
        summed = jnp.dot(
            weights.astype(bf16).reshape(GROUP * PAD, tokens), values, preferred_element_type=f32
        ).reshape(GROUP, PAD, HEAD)
        attended = (summed + own_weight * new_value[None]) / total
        for g in range(GROUP):
            at = slice(base + g * HEAD, base + (g + 1) * HEAD)
            residual = res_ref[:, pl.ds(start + g * HEAD, HEAD)].astype(f32)
            mixed = residual + attended[g][:slots]
            mixed_refs[job[0]][:, at] = mixed
            squares = squares + mixed * mixed
            gain = gain_ref[pl.ds(block * (step // HEAD) + job[1] * GROUP + g, 1), :]
            gained = pad_rows((mixed * gain).astype(bf16))
            rows = jnp.dot(pick, gained, preferred_element_type=f32)
            counted = lax.broadcasted_iota(i32, rows.shape, 0) == PAD - 1
            sends[job[0]][:, at] = jnp.where(counted, count.astype(f32), rows).astype(bf16)
    square_ref[...] = squares


def attend(inputs, side, sides, masks, before):
    queries, new_kv, kv_pool, page_table, ctx_len, residual_in, norm_gain = inputs
    slots, columns = queries.shape
    pages, page, _ = kv_pool.shape
    step = columns // sides
    first = before is None
    vmem, anywhere = pl.BlockSpec(memory_space=pltpu.VMEM), pl.BlockSpec(memory_space=pl.ANY)
    smem = pl.BlockSpec(memory_space=pltpu.SMEM)
    out_shape = [jax.ShapeDtypeStruct((PAD, step), bf16)] * len(masks)
    out_shape += [jax.ShapeDtypeStruct((slots, step), f32)] * len(masks)
    out_shape += [jax.ShapeDtypeStruct((slots, HEAD), f32)]
    if first:
        operands = [page_table, queries, new_kv, residual_in, norm_gain, kv_pool]
        in_specs = [vmem] + [anywhere] * 5
        out_shape += [
            pltpu.VMEM(queries.shape, bf16),
            pltpu.VMEM(new_kv.shape, bf16),
            pltpu.VMEM(residual_in.shape, bf16),
            pltpu.VMEM(norm_gain.shape, f32),
            pltpu.VMEM((PAD, pages * page), f32),
        ]
        scratch = [pltpu.VMEM(norm_gain.shape, bf16), pltpu.SemaphoreType.DMA((4,))]
    else:
        operands = [*before, kv_pool]
        in_specs = [vmem] * len(before) + [anywhere]
        scratch = []
    scratch += [
        pltpu.VMEM((pages, page, kv_pool.shape[2] // sides * 2), bf16),
        pltpu.SemaphoreType.DMA((2, POOL_CUTS)),
    ]
    outs = pl.pallas_call(
        functools.partial(attend_kernel, masks=masks, sides=sides, first=first),
        in_specs=[smem, smem] + in_specs,
        out_specs=[vmem] * len(out_shape),
        out_shape=out_shape,
        scratch_shapes=scratch,
        compiler_params=params(28),
        cost_estimate=cost(2e9, kv_pool.size),
        name="attend",
    )(ctx_len, side, *operands)
    n = len(masks)
    return outs[:n], outs[n : 2 * n], outs[2 * n], outs[2 * n + 1 :]


UP_TILE = 256
DOWN_TILE = 512


def tile_copy(w_ref, row, rows, column, buffer, sems, t, tile):
    at = pl.ds(pl.multiple_of(t * tile, tile), tile)
    source = w_ref.at[pl.ds(row, rows), pl.ds(pl.multiple_of(column + t * tile, tile), tile)]
    return pltpu.make_async_copy(source, buffer.at[:, at], sems.at[t])


def up_kernel(side, x_ref, w_ref, out_ref, buffer, sems, *, masks):
    depth, width = buffer.shape[1:]
    tiles = width // UP_TILE

    def copy_of(n, t):
        column = pl.multiple_of(((side[0] ^ masks[n][0]) * 2 + masks[n][1]) * width, width)
        return tile_copy(w_ref, 0, depth, column, buffer.at[n], sems.at[n], t, UP_TILE)

    for n in range(len(masks)):
        for t in range(tiles):
            copy_of(n, t).start()

    @pl.loop(0, len(masks) * tiles)
    def _(job):
        n, t = lax.div(job, tiles), lax.rem(job, tiles)
        at = pl.ds(pl.multiple_of(t * UP_TILE, UP_TILE), UP_TILE)
        pltpu.make_async_copy(
            w_ref.at[:, pl.ds(0, UP_TILE)], buffer.at[n, :, at], sems.at[n, t]
        ).wait()
        out_ref[n, :, at] = jnp.dot(
            x_ref[: out_ref.shape[1], :], buffer[n, :, at], preferred_element_type=f32
        ).astype(out_ref.dtype)


def up(side, packed, w_up, rows, width, masks):
    depth = packed.shape[1]
    vmem, smem = pl.BlockSpec(memory_space=pltpu.VMEM), pl.BlockSpec(memory_space=pltpu.SMEM)
    return pl.pallas_call(
        functools.partial(up_kernel, masks=masks),
        in_specs=[smem, vmem, pl.BlockSpec(memory_space=pl.ANY)],
        out_specs=vmem,
        out_shape=jax.ShapeDtypeStruct((len(masks), rows, width), bf16),
        scratch_shapes=[
            pltpu.VMEM((len(masks), depth, width), bf16),
            pltpu.SemaphoreType.DMA((len(masks), width // UP_TILE)),
        ],
        compiler_params=params(24),
        cost_estimate=cost(2 * rows * depth * width, depth * width * 2 * len(masks)),
        name="up",
    )(side, packed, w_up)


PIECES = ((0, 2), (1, 3))


def find_layout(side, shard, gathered, layout, step_ref, limits):
    pieces = gathered[0].shape[0] // PAD
    devices = len(gathered) * pieces
    counts, places = [None] * devices, [None] * devices
    for part in range(len(gathered)):
        for piece, mask in enumerate(PIECES[part % 2]):
            last = gathered[part][piece * PAD : (piece + 1) * PAD, :HEAD].astype(f32)[PAD - 1 :]
            place = part // 2 * 4 + mask
            counts[place] = jnp.max(last).astype(i32)
            places[place] = (side[0] ^ mask) * 4 + (shard[0] ^ (part // 2))
    total = jnp.int32(0)
    for one in range(devices):
        base = jnp.int32(0)
        for other in range(devices):
            base = base + jnp.where(places[other] < places[one], counts[other], 0)
        layout[one] = base
        layout[devices + one] = counts[one]
        total = total + counts[one]
    step = jnp.int32(0)
    for limit in limits:
        step = step + (total > limit).astype(i32)
    step_ref[0] = step


def pack_up_kernel(side, shard, *refs, mask, limits):
    gathered, refs = refs[:-7], refs[-7:]
    w_ref, packed_ref, out_ref, layout, step_ref, buffer, sems = refs
    width = out_ref.shape[1]

    def copy_of(t):
        column = pl.multiple_of((side[0] ^ mask) * 2 * width, width)
        return tile_copy(w_ref, 0, buffer.shape[0], column, buffer, sems, t, UP_TILE)

    for t in range(width // UP_TILE):
        copy_of(t).start()
    find_layout(side, shard, gathered, layout, step_ref, limits)
    rows, depth = packed_ref.shape
    per = gathered[0].shape[0]
    lane = lax.broadcasted_iota(i32, (rows, per), 1)
    row = lax.broadcasted_iota(i32, (rows, per), 0)
    devices = len(gathered) * (per // PAD)
    picks = []
    for part in range(len(gathered)):
        target = jnp.full((rows, per), -1, i32)
        for piece, mask in enumerate(PIECES[part % 2]):
            place = part // 2 * 4 + mask
            base, count = layout[place], layout[devices + place]
            inside = lane - piece * PAD
            mine = jnp.logical_and(inside >= 0, inside < count)
            target = jnp.where(mine, base + inside, target)
        picks.append((target == row).astype(f32).astype(bf16))
    pick = jnp.concatenate(picks, axis=1)

    @pl.loop(0, depth // DOWN_TILE)
    def _(t):
        at = pl.ds(pl.multiple_of(t * DOWN_TILE, DOWN_TILE), DOWN_TILE)
        pieces = jnp.concatenate([part[:, at] for part in gathered], axis=0)
        packed_ref[:, at] = jnp.dot(pick, pieces, preferred_element_type=f32).astype(bf16)

    @pl.loop(0, width // UP_TILE)
    def _(t):
        copy_of(t).wait()
        at = pl.ds(pl.multiple_of(t * UP_TILE, UP_TILE), UP_TILE)
        out_ref[:, at] = jnp.dot(
            packed_ref[...], buffer[:, at], preferred_element_type=f32
        ).astype(bf16)


def pack_up(side, shard, gathered, w_up, rows, width, mask, limits):
    depth = w_up.shape[0]
    devices = len(gathered) * gathered[0].shape[0] // PAD
    vmem, smem = pl.BlockSpec(memory_space=pltpu.VMEM), pl.BlockSpec(memory_space=pltpu.SMEM)
    return pl.pallas_call(
        functools.partial(pack_up_kernel, mask=mask, limits=limits),
        in_specs=[smem, smem] + [vmem] * len(gathered) + [pl.BlockSpec(memory_space=pl.ANY)],
        out_specs=[vmem, vmem, smem, smem],
        out_shape=[
            jax.ShapeDtypeStruct((rows, depth), bf16),
            jax.ShapeDtypeStruct((rows, width), bf16),
            jax.ShapeDtypeStruct((2 * devices,), i32),
            jax.ShapeDtypeStruct((1,), i32),
        ],
        scratch_shapes=[
            pltpu.VMEM((depth, width), bf16),
            pltpu.SemaphoreType.DMA((width // UP_TILE,)),
        ],
        compiler_params=params(24),
        cost_estimate=cost(2 * rows * depth * width, depth * width * 2),
        name="pack_up",
    )(side, shard, *gathered, w_up)


def down_kernel(side, *refs, first, mask, ahead):
    refs = list(refs)
    a_ref, w_ref = refs.pop(0), refs.pop(0)
    before_ref = None if first else refs.pop(0)
    out_ref = refs.pop(0)
    next_ref = refs.pop(0) if ahead is not None else None
    buffer, sems = refs.pop(0), refs.pop(0)
    depth, width = buffer.shape
    tiles = width // DOWN_TILE

    def copy_of(other, buffer, sems, t):
        row = pl.multiple_of((side[0] ^ other) * depth, depth)
        return tile_copy(w_ref, row, depth, 0, buffer, sems, t, DOWN_TILE)

    for t in range(tiles):
        copy_of(mask, buffer, sems, t).start()
    if ahead is not None:
        for t in range(tiles):
            copy_of(ahead, next_ref, refs[0], t).start()

    @pl.loop(0, tiles)
    def _(t):
        at = pl.ds(pl.multiple_of(t * DOWN_TILE, DOWN_TILE), DOWN_TILE)
        copy_of(mask, buffer, sems, t).wait()
        part = jnp.dot(a_ref[...], buffer[:, at], preferred_element_type=f32)
        out_ref[:, at] = part if first else before_ref[:, at] + part

    if ahead is not None:

        @pl.loop(0, tiles)
        def _(t):
            copy_of(ahead, next_ref, refs[0], t).wait()


def down(side, active, w_down, before, mask, ahead=None):
    rows, depth = active.shape
    width = w_down.shape[1]
    vmem, smem = pl.BlockSpec(memory_space=pltpu.VMEM), pl.BlockSpec(memory_space=pltpu.SMEM)
    out = jax.ShapeDtypeStruct((rows, width), f32)
    sems = pltpu.SemaphoreType.DMA((width // DOWN_TILE,))
    return pl.pallas_call(
        functools.partial(down_kernel, first=before is None, mask=mask, ahead=ahead),
        in_specs=[smem, vmem, pl.BlockSpec(memory_space=pl.ANY)]
        + ([] if before is None else [vmem]),
        out_specs=vmem if ahead is None else [vmem, vmem],
        out_shape=out if ahead is None else [out, pltpu.VMEM((depth, width), bf16)],
        scratch_shapes=[pltpu.VMEM((depth, width), bf16), sems]
        + ([] if ahead is None else [sems]),
        compiler_params=params(24),
        cost_estimate=cost(2 * rows * depth * width, depth * width * 2),
        name="down",
    )(side, active, w_down, *([] if before is None else [before]))


BACK = ((2, 3), (0, 1))


def down_unpack_kernel(layout, a_ref, w_ref, before_ref, *refs):
    outs, wide = refs[:-1], refs[-1]
    rows = a_ref.shape[0]
    tiles, devices = wide.shape[:2]
    group = devices // len(outs)
    row = lax.broadcasted_iota(i32, (PAD, rows), 0)
    column = lax.broadcasted_iota(i32, (PAD, rows), 1)
    picks = []
    for core in (0, 1):
        for x in (2, 0):
            for masks in BACK:
                for mask in masks:
                    place = (x + core) * 4 + mask
                    base, count = layout[place], layout[devices + place]
                    picks.append(jnp.logical_and(column - row == base, row < count).astype(f32))
    pick = jnp.concatenate(picks, axis=0).astype(bf16)

    @pl.loop(0, tiles)
    def _(t):
        at = pl.ds(pl.multiple_of(t * DOWN_TILE, DOWN_TILE), DOWN_TILE)
        share = before_ref[:, at] + jnp.dot(a_ref[...], w_ref[:, at], preferred_element_type=f32)
        back = jnp.dot(pick, share.astype(bf16), preferred_element_type=f32)
        wide[t] = back.reshape(devices, PAD, DOWN_TILE)

    per = tiles * LIVE_CAP
    for n, out in enumerate(outs):

        @pl.loop(0, group)
        def _(device):
            here = [wide[t, n * group + device, :LIVE_CAP, :] for t in range(tiles)]
            rows = pl.ds(pl.multiple_of(device * per, per), per)
            out[rows, :] = jnp.concatenate(here, axis=0).astype(bf16)


def down_unpack(layout, active, weights, before):
    rows, depth = active.shape
    width = weights.shape[1]
    tiles, devices = width // DOWN_TILE, layout.shape[0] // 2
    vmem, smem = pl.BlockSpec(memory_space=pltpu.VMEM), pl.BlockSpec(memory_space=pltpu.SMEM)
    out = jax.ShapeDtypeStruct((devices // 2 * tiles * LIVE_CAP, DOWN_TILE), bf16)
    return pl.pallas_call(
        down_unpack_kernel,
        in_specs=[smem, vmem, vmem, vmem],
        out_specs=[vmem] * 2,
        out_shape=[out] * 2,
        scratch_shapes=[pltpu.VMEM((tiles, devices, PAD, DOWN_TILE), f32)],
        compiler_params=params(24),
        cost_estimate=cost(2 * rows * depth * width, rows * width * 4),
        name="down_unpack",
    )(layout, active, weights, before)


def finish_kernel(lengths, side, *refs):
    out_ref = refs[-1]
    sides = (len(refs) - 3) // 2
    mixed, squares, blocks = refs[:sides], refs[sides : sides + 2], refs[sides + 2 : -1]
    slots, width = out_ref.shape
    step = width // sides
    total = squares[0][...] + squares[1][...]
    root = lax.rsqrt(jnp.sum(total, axis=-1, keepdims=True) / width + epsilon)
    gain = root * root
    tiles = step // DOWN_TILE
    picks = [
        live_pick(lengths, slots, tiles * LIVE_CAP, t * LIVE_CAP, True)[0] for t in range(tiles)
    ]
    for shift in range(sides):
        base = (side[0] ^ shift) * step
        block = blocks[shift][...]
        for t in range(tiles):
            back = jnp.dot(picks[t], block, preferred_element_type=f32)[:slots]
            at = pl.multiple_of(base + t * DOWN_TILE, DOWN_TILE)
            here = mixed[shift][:, t * DOWN_TILE : (t + 1) * DOWN_TILE]
            out_ref[:, pl.ds(at, DOWN_TILE)] = (here + gain * back).astype(bf16)


def finish(ctx_len, side, mixed, squares, blocks):
    vmem, smem = pl.BlockSpec(memory_space=pltpu.VMEM), pl.BlockSpec(memory_space=pltpu.SMEM)
    slots, width = mixed[0].shape[0], mixed[0].shape[1] * len(mixed)
    return pl.pallas_call(
        finish_kernel,
        in_specs=[smem, smem] + [vmem] * (2 * len(mixed) + 2),
        out_specs=vmem,
        out_shape=jax.ShapeDtypeStruct((slots, width), bf16),
        compiler_params=params(16),
        cost_estimate=cost(slots * width * 32, slots * width * 8),
        name="finish",
    )(ctx_len, side, *mixed, *squares, *blocks)


def swap(x, axis, count, mask):
    return lax.ppermute(x, axis, [(j, j ^ mask) for j in range(count)])


def added(a, b):
    return (a.astype(f32) + b.astype(f32)).astype(bf16)


def tie(x, *others):
    return lax.optimization_barrier((x, *others))[0]


def squared_relu(*terms):
    lifted = sum(term.astype(f32) for term in terms)
    clipped = jnp.maximum(lifted, 0.0)
    return (clipped * clipped).astype(bf16)


def feed_forward(rows, side, layout, packed, other, w_up, w_down):
    half = w_up.shape[1] // 8
    across = lambda x: swap(x, "side", 4, 2)
    beside = lambda x: swap(x, "side", 4, 1)
    met_0 = beside(other[:rows])
    far = up(side, packed, w_up, rows, half, ((3, 1), (2, 0), (2, 1)))
    met_1 = beside(far[0])
    sum_0 = added(far[1], met_0)
    crossed_0 = across(sum_0)
    near = up(side, tie(packed, sum_0), w_up, rows, half, ((1, 0), (1, 1)))
    met_1, near = lax.optimization_barrier((met_1, near))
    sum_1 = added(far[2], met_1)
    crossed_1 = across(sum_1)
    near = beside(near)
    own = up(side, tie(packed, sum_1), w_up, rows, half, ((0, 0), (0, 1)))
    active = [squared_relu(own[n], near[n], crossed) for n, crossed in enumerate((crossed_0, crossed_1))]
    active = jnp.concatenate(active, axis=1)
    over, following = across(active), beside(active)
    total = down(side, active, w_down, None, 0)
    forward = beside(tie(over, total))
    total = down(side, following, w_down, total, 1)
    total, weights = down(side, over, w_down, total, 2, ahead=3)
    return down_unpack(layout, forward, weights, total)


ROW_STEPS = (112, 120, 128, 136, 144, 160, 192)


def line_shards(
    queries, new_kv, kv_pool, page_table, ctx_len, residual_in, norm_gain, w_up, w_down
):
    i, s = lax.axis_index("side"), lax.axis_index("shard")
    side, shard = i.reshape(1), s.reshape(1)
    in_hbm = lambda x: pltpu.with_memory_space_constraint(x, pltpu.HBM)
    gain = norm_gain.reshape(-1, HEAD)
    inputs = queries, new_kv, kv_pool, page_table, ctx_len, residual_in, gain
    inputs, w_up, w_down = jax.tree.map(in_hbm, (inputs, w_up, w_down))
    ctx_len = inputs[4]
    (to_2, to_3), mixed_far, squares_far, copies = attend(inputs, side, 4, (2, 3), None)
    met = swap(jnp.concatenate([to_2, to_3], axis=0), "side", 4, 2)
    (own, to_1), mixed_near, squares_near, _ = attend(inputs, side, 4, (0, 1), copies)
    first = jnp.concatenate([own, met[:PAD]], axis=0)
    second = swap(jnp.concatenate([to_1, met[PAD:]], axis=0), "side", 4, 1)
    gathered = []
    by_x = [swap(here, "shard", 4, 2) for here in (first, second)]
    by_core = [swap(here, "shard", 4, 1) for here in (first, second)]
    by_both = [swap(there, "shard", 4, 1) for there in by_x]
    gathered = [first, second, *by_core, *by_x, *by_both]
    packed, other, layout, step = pack_up(
        side, shard, gathered, w_up, ROW_STEPS[-1], w_up.shape[1] // 8, 3, ROW_STEPS[:-1]
    )
    stay, leave = lax.switch(
        step[0],
        [functools.partial(feed_forward, rows) for rows in ROW_STEPS],
        side, layout, packed, other, w_up, w_down,
    )
    back = swap(leave, "shard", 4, 1)
    quarter = back.shape[0] // 4
    piece = quarter // 2
    cuts = [slice(at, at + quarter) for at in range(0, 4 * quarter, quarter)]
    sums = [added(stay[cut], back[cut]) for cut in cuts]
    far = added(sums[2], swap(sums[0], "shard", 4, 2))
    near = added(sums[3], swap(sums[1], "shard", 4, 2))
    home = near[:piece], near[piece:], far[:piece], far[piece:]
    blocks = [home[0]] + [swap(home[mask], "side", 4, mask) for mask in (1, 2, 3)]
    mixed = [*mixed_near, *mixed_far]
    return finish(ctx_len, side, mixed, [squares_far, squares_near], blocks)


def attend_slots(queries, new_kv, pool_pages, page_rows, lengths):
    slot_count = queries.shape[0]
    positions = page_rows.shape[1] * pool_pages.shape[1]
    fetched = pool_pages[page_rows].reshape(slot_count, positions, 2, KV_HEADS, HEAD)
    fresh_kv = new_kv.reshape(slot_count, 2, KV_HEADS, HEAD)
    query_heads = queries.reshape(slot_count, KV_HEADS, GROUP, HEAD)
    score_scale = 1.0 / math.sqrt(HEAD)
    scores = (
        jnp.einsum("sgqd,slgd->sgql", query_heads, fetched[:, :, 0], preferred_element_type=f32)
        * score_scale
    )
    own_score = (
        jnp.einsum("sgqd,sgd->sgq", query_heads, fresh_kv[:, 0], preferred_element_type=f32)
        * score_scale
    )
    visible = (jnp.arange(positions, dtype=i32)[None, :] < lengths[:, None])[:, None, None, :]
    scores = jnp.where(visible, scores, -1e30)
    highest = jnp.maximum(jnp.max(scores, axis=-1), own_score)
    weights = jnp.where(visible, jnp.exp(scores - highest[..., None]), 0.0)
    own_weight = jnp.exp(own_score - highest)
    denominator = jnp.sum(weights, axis=-1) + own_weight
    probabilities = (weights / denominator[..., None]).astype(bf16)
    own_prob = (own_weight / denominator).astype(bf16).astype(f32)
    attended = jnp.einsum(
        "sgql,slgd->sgqd", probabilities, fetched[:, :, 1], preferred_element_type=f32
    )
    attended = attended + own_prob[..., None] * fresh_kv[:, 1].astype(f32)[:, :, None, :]
    return attended.reshape(slot_count, -1)


def any_shards(queries, new_kv, kv_pool, page_table, ctx_len, residual_in, norm_gain, w_up, w_down):
    attended = attend_slots(queries, new_kv, kv_pool, page_table, ctx_len)
    mixed_rows = residual_in.astype(f32) + attended
    mean_square = jnp.mean(mixed_rows * mixed_rows, axis=-1, keepdims=True)
    normed = (mixed_rows * lax.rsqrt(mean_square + epsilon) * norm_gain.astype(f32)).astype(bf16)
    live_mask = ctx_len > 0
    spread = lax.all_to_all(normed, "side", split_axis=1, concat_axis=0, tiled=True)
    up_partial = jnp.dot(
        lax.all_gather(spread, "shard", axis=0, tiled=True), w_up, preferred_element_type=f32
    )
    lifted = lax.psum(up_partial, "side")
    clipped = jnp.maximum(lifted, 0.0)
    active = (clipped * clipped).astype(bf16)
    down_share = lax.psum_scatter(
        jnp.dot(active, w_down, preferred_element_type=f32).astype(bf16),
        "shard",
        scatter_dimension=0,
        tiled=True,
    )
    returned = lax.all_to_all(down_share, "side", split_axis=0, concat_axis=1, tiled=True)
    returned = jnp.where(live_mask[:, None], returned.astype(f32), 0.0)
    return (mixed_rows + returned).astype(bf16)


def solution(mesh):
    rows = ("grp", "side", "shard")
    placed = (
        P(rows, None),
        P(rows, None),
        P(rows, None, None),
        P(rows, None),
        P(rows),
        P(rows, None),
        P(),
        P("side", "shard"),
        P("shard", "side"),
    )
    square = mesh.shape["side"] == 4 and mesh.shape["shard"] == 4
    return jax.shard_map(
        line_shards if square else any_shards,
        mesh=mesh,
        in_specs=placed,
        out_specs=P(rows, None),
        check_vma=False,
    )
```

profile of v0, /device:TPU:0, one launch (start us, length us, event | category | flops | bytes accessed | tf_op | source)
XLA Modules:
  0.0 96.2 jit_solution(7761958608701313059)
XLA Ops:
  0.0 5.6 %attend.2 = (bf16[16,2048]{1,0:T(8,128)(2,1)S(1)}, bf16[16,2048]{1,0:T(8,128)(2,1)S(1)}, f32[15,2048]{1,0:T(8,128)S(1)}, f32[15,2048]{1,0:T(8,128)S(1)}, f32[15,...) custom-call(s32[15]{0:T(128)} %lengths.5, ...), custom_call_target="tpu_custom_call" | custom-call | flops 31250000 | bytes 57344 | tf_op jit(solution)/shard_map/attend/pallas_call | solution.py:230
  5.6 4.1 %collective-permute-start.56 = (bf16[32,2048]{1,0:T(8,128)(2,1)S(1)}, bf16[32,2048]{1,0:T(8,128)(2,1)S(1)}, u32[]{:S(2)}, u32[]{:S(2)}) collective-permute-start(bf16[32,2048]{1,0:T(8,128)(2,1)S(1)} %pad_maximum_fusion.7), channel_id=1, source_target_pairs={{0,8},{4,12},{8,0},{12,4},{1,9},{5,13},{9,1},{13,5},{2,10},{6,14},... | collective-permute-start | bytes 393224 | tf_op jit(solution)/shard_map/ppermute | solution.py:538
  9.7 4.8 %attend.3 = (bf16[16,2048]{1,0:T(8,128)(2,1)S(1)}, bf16[16,2048]{1,0:T(8,128)(2,1)S(1)}, f32[15,2048]{1,0:T(8,128)S(1)}, f32[15,2048]{1,0:T(8,128)S(1)}, f32[15,128]{1,0:T(8,128)S(1)}) custom-call(s32[15]{0:T(128)} %lengths.5, s32[1]{0:T(128)} %bitcast.49.side, bf16[15,8192]{1,0:T(8,128)(2,1)S(1)} %get-tuple-element.201.refs_0_, ...), custom_call_target="tpu_custom_call" | custom-call | flops 31250000 | bytes 57344 | tf_op jit(solution)/shard_map/attend/pallas_call | solution.py:230
  14.5 1.5 %collective-permute-done.56 = bf16[32,2048]{1,0:T(8,128)(2,1)S(1)} collective-permute-done((bf16[32,2048]{1,0:T(8,128)(2,1)S(1)}, bf16[32,2048]{1,0:T(8,128)(2,1)S(1)}, u32[]{:S(2)}, u32[]{:S(2)}) %collective-permute-start.56) | collective-permute-done | bytes 131104 | tf_op jit(solution)/shard_map/ppermute | solution.py:538
  16.1 0.8 collective-permute-start.57
  16.9 1.6 %collective-permute-start.60 = (bf16[32,2048]{1,0:T(8,128)(2,1)S(1)}, bf16[32,2048]{1,0:T(8,128)(2,1)S(1)}, u32[]{:S(2)}, u32[]{:S(2)}) collective-permute-start(bf16[32,2048]{1,0:T(8,128)(2,1)S(1)} %pad_maximum_fusion.8.refs_0_), channel_id=1, source_target_pairs={{0,2},{1,3},{2,0},{3,1},{4,6},{5,7},{6,4},{7,5},{8,10},{9,11},{10,... | collective-permute-start | bytes 393224 | tf_op jit(solution)/shard_map/ppermute | solution.py:538
  18.4 2.7 %collective-permute-done.57.refs_1_ = bf16[32,2048]{1,0:T(8,128)(2,1)S(1)} collective-permute-done((bf16[32,2048]{1,0:T(8,128)(2,1)S(1)}, bf16[32,2048]{1,0:T(8,128)(2,1)S(1)}, u32[]{:S(2)}, u32[]{:S(2)}) %collective-permute-start.57) | collective-permute-done | bytes 131104 | tf_op jit(solution)/shard_map/ppermute | solution.py:538
  21.1 1.5 %collective-permute-start.61 = (bf16[32,2048]{1,0:T(8,128)(2,1)S(1)}, bf16[32,2048]{1,0:T(8,128)(2,1)S(1)}, u32[]{:S(2)}, u32[]{:S(2)}) collective-permute-start(bf16[32,2048]{1,0:T(8,128)(2,1)S(1)} %collective-permute-done.57.refs_1_), channel_id=1, source_target_pairs={{0,2},{1,3},{2,0},{3,1},{4,6},{5,7},{6,4},{7,5},{8,10},{9,11},{10,... | collective-permute-start | bytes 393224 | tf_op jit(solution)/shard_map/ppermute | solution.py:538
  22.6 0.0 collective-permute-start.58
  22.6 0.5 collective-permute-start.59
  23.1 0.0 collective-permute-start.62
  23.1 2.9 %collective-permute-done.61.refs_5_ = bf16[32,2048]{1,0:T(8,128)(2,1)S(1)} collective-permute-done((bf16[32,2048]{1,0:T(8,128)(2,1)S(1)}, bf16[32,2048]{1,0:T(8,128)(2,1)S(1)}, u32[]{:S(2)}, u32[]{:S(2)}) %collective-permute-start.61) | collective-permute-done | bytes 131104 | tf_op jit(solution)/shard_map/ppermute | solution.py:538
  26.1 1.3 %collective-permute-done.63.refs_7_ = bf16[32,2048]{1,0:T(8,128)(2,1)S(1)} collective-permute-done((bf16[32,2048]{1,0:T(8,128)(2,1)S(1)}, bf16[32,2048]{1,0:T(8,128)(2,1)S(1)}, u32[]{:S(2)}, u32[]{:S(2)}) %collective-permute-start.63) | collective-permute-done | bytes 131104 | tf_op jit(solution)/shard_map/ppermute | solution.py:538
  27.4 2.8 %pack_up.1 = (bf16[192,2048]{1,0:T(8,128)(2,1)S(1)}, bf16[192,512]{1,0:T(8,128)(2,1)S(1)}, s32[32]{0:T(128)S(1)}, s32[1]{0:T(128)}) custom-call(s32[1]{0:T(128)} %bitcast.49.side, s32[1]{0:T(128)} %bitcast.51.shard, bf16[32,2048]{1,0:T(8,128)(2,1)S(1)} %pad_maximum_fusion.8.refs_0_, bf16[32,2048]{1,0:T(8,128)(2,1)S(1)} %collective-permute-done.57.refs_1_, ...), custom_call_target="tpu_custom_call" | custom-call | flops 6291456 | bytes 32768 | tf_op jit(solution)/shard_map/pack_up/pallas_call | solution.py:371
  30.8 45.7 %conditional.1 = ((bf16[384,512]{1,0:T(8,128)(2,1)S(1)}, bf16[384,512]{1,0:T(8,128)(2,1)S(1)})) conditional(s32[]{:T(128)} %bitcast.52, (s32[1]{0:T(128)}, bf16[192,2048]{1,0:T(8,128)(2,1)S(1)}, bf16[2048,4096]{1,0:T(8,128)(2,1)}, bf16[192,512]{1,0:T(8,128)(2,1)S(1)}, bf16[4096,2048]{1,0:T(8,128)(2,1)}, ...), branch_computations={%region_0.0_spmd, %region_1.0_spmd, %region_2.0_spmd, %region_3.0_... | conditional | flops 72351744 | bytes 13820232 | solution.py:606
  31.1 1.2 %collective-permute-start.17 = (bf16[128,512]{1,0:T(8,128)(2,1)S(1)}, bf16[128,512]{1,0:T(8,128)(2,1)S(1)}, u32[]{:S(2)}, u32[]{:S(2)}) collective-permute-start(bf16[128,512]{1,0:T(8,128)(2,1)S(1)} %slice.157), channel_id=1, source_target_pairs={{0,4},{4,0},{8,12},{12,8},{1,5},{5,1},{9,13},{13,9},{2,6},{6,2},{1... | collective-permute-start | bytes 393224 | tf_op jit(solution)/shard_map/cond/branch_2_fun/ppermute | solution.py:538
  32.3 3.2 %up.27 = bf16[3,128,512]{2,1,0:T(8,128)(2,1)S(1)} custom-call(s32[1]{0:T(128)} %get-tuple-element.116.side, bf16[192,2048]{1,0:T(8,128)(2,1)S(1)} %get-tuple-element.122.x_ref, bf16[2048,4096]{1,0:T(8,128)(2,1)} %get-tuple-element.118.w_ref), custom_call_target="tpu_custom_call" | custom-call | flops 4194304 | bytes 98304 | tf_op jit(solution)/shard_map/cond/branch_2_fun/up/pallas_call | solution.py:281
  35.6 0.9 collective-permute-start.16
  36.5 0.2 collective-permute-done.17
  36.7 2.9 %collective-permute-start.19 = (bf16[128,512]{1,0:T(8,128)(2,1)S(1)}, bf16[128,512]{1,0:T(8,128)(2,1)S(1)}, u32[]{:S(2)}, u32[]{:S(2)}) collective-permute-start(bf16[128,512]{1,0:T(8,128)(2,1)S(1)} %fusion.16), channel_id=1, source_target_pairs={{0,8},{4,12},{8,0},{12,4},{1,9},{5,13},{9,1},{13,5},{2,10},{6,14},... | collective-permute-start | bytes 393224 | tf_op jit(solution)/shard_map/cond/branch_2_fun/ppermute | solution.py:538
  39.6 2.6 %up.28 = bf16[2,128,512]{2,1,0:T(8,128)(2,1)S(1)} custom-call(s32[1]{0:T(128)} %get-tuple-element.116.side, bf16[192,2048]{1,0:T(8,128)(2,1)S(1)} %get-tuple-element.122.x_ref, bf16[2048,4096]{1,0:T(8,128)(2,1)} %get-tuple-element.118.w_ref), custom_call_target="tpu_custom_call" | custom-call | flops 4194304 | bytes 65536 | tf_op jit(solution)/shard_map/cond/branch_2_fun/up/pallas_call | solution.py:281
  42.2 1.5 %collective-permute-done.16 = bf16[128,512]{1,0:T(8,128)(2,1)S(1)} collective-permute-done((bf16[128,512]{1,0:T(8,128)(2,1)S(1)}, bf16[128,512]{1,0:T(8,128)(2,1)S(1)}, u32[]{:S(2)}, u32[]{:S(2)}) %collective-permute-start.16) | collective-permute-done | bytes 131104 | tf_op jit(solution)/shard_map/cond/branch_2_fun/ppermute | solution.py:538
  43.7 0.3 collective-permute-start.18
  44.0 1.5 %collective-permute-start.20 = (bf16[128,512]{1,0:T(8,128)(2,1)S(1)}, bf16[128,512]{1,0:T(8,128)(2,1)S(1)}, u32[]{:S(2)}, u32[]{:S(2)}) collective-permute-start(bf16[128,512]{1,0:T(8,128)(2,1)S(1)} %fusion.17), channel_id=1, source_target_pairs={{0,8},{4,12},{8,0},{12,4},{1,9},{5,13},{9,1},{13,5},{2,10},{6,14},... | collective-permute-start | bytes 393224 | tf_op jit(solution)/shard_map/cond/branch_2_fun/ppermute | solution.py:538
  45.5 2.6 %up.29 = bf16[2,128,512]{2,1,0:T(8,128)(2,1)S(1)} custom-call(s32[1]{0:T(128)} %get-tuple-element.116.side, bf16[192,2048]{1,0:T(8,128)(2,1)S(1)} %get-tuple-element.122.x_ref, bf16[2048,4096]{1,0:T(8,128)(2,1)} %get-tuple-element.118.w_ref), custom_call_target="tpu_custom_call" | custom-call | flops 4194304 | bytes 65536 | tf_op jit(solution)/shard_map/cond/branch_2_fun/up/pallas_call | solution.py:281
  48.1 3.6 %collective-permute-done.20 = bf16[128,512]{1,0:T(8,128)(2,1)S(1)} collective-permute-done((bf16[128,512]{1,0:T(8,128)(2,1)S(1)}, bf16[128,512]{1,0:T(8,128)(2,1)S(1)}, u32[]{:S(2)}, u32[]{:S(2)}) %collective-permute-start.20) | collective-permute-done | bytes 131104 | tf_op jit(solution)/shard_map/cond/branch_2_fun/ppermute | solution.py:538
  51.6 0.8 collective-permute-done.18
  52.5 0.1 fusion.23
  52.6 2.6 %collective-permute-start.21 = (bf16[128,1024]{1,0:T(8,128)(2,1)S(1)}, bf16[128,1024]{1,0:T(8,128)(2,1)S(1)}, u32[]{:S(2)}, u32[]{:S(2)}) collective-permute-start(bf16[128,1024]{1,0:T(8,128)(2,1)S(1)} %pad_maximum_fusion.2.refs_0_), channel_id=1, source_target_pairs={{0,8},{4,12},{8,0},{12,4},{1,9},{5,13},{9,1},{13,5},{2,10},{6,14},... | collective-permute-start | bytes 786440 | tf_op jit(solution)/shard_map/cond/branch_2_fun/ppermute | solution.py:538
  55.3 2.3 %collective-permute-start.23 = (bf16[128,1024]{1,0:T(8,128)(2,1)S(1)}, bf16[128,1024]{1,0:T(8,128)(2,1)S(1)}, u32[]{:S(2)}, u32[]{:S(2)}) collective-permute-start(bf16[128,1024]{1,0:T(8,128)(2,1)S(1)} %pad_maximum_fusion.2.refs_0_), channel_id=1, source_target_pairs={{0,4},{4,0},{8,12},{12,8},{1,5},{5,1},{9,13},{13,9},{2,6},{6,2},{1... | collective-permute-start | bytes 786440 | tf_op jit(solution)/shard_map/cond/branch_2_fun/ppermute | solution.py:538
  57.5 2.6 %down.27.refs_2_ = f32[128,2048]{1,0:T(8,128)S(1)} custom-call(s32[1]{0:T(128)} %get-tuple-element.116.side, bf16[128,1024]{1,0:T(8,128)(2,1)S(1)} %pad_maximum_fusion.2.refs_0_, bf16[4096,2048]{1,0:T(8,128)(2,1)} %get-tuple-element.124.refs_1_), custom_call_target="tpu_custom_call" | custom-call | flops 8388608 | bytes 65536 | tf_op jit(solution)/shard_map/cond/branch_2_fun/down/pallas_call | solution.py:431
  60.1 6.3 %collective-permute-done.21.refs_0_ = bf16[128,1024]{1,0:T(8,128)(2,1)S(1)} collective-permute-done((bf16[128,1024]{1,0:T(8,128)(2,1)S(1)}, bf16[128,1024]{1,0:T(8,128)(2,1)S(1)}, u32[]{:S(2)}, u32[]{:S(2)}) %collective-permute-start.21) | collective-permute-done | bytes 262176 | tf_op jit(solution)/shard_map/cond/branch_2_fun/ppermute | solution.py:538
  66.4 0.7 collective-permute-start.22
  67.0 2.5 %down.28.refs_2_ = f32[128,2048]{1,0:T(8,128)S(1)} custom-call(s32[1]{0:T(128)} %get-tuple-element.116.side, bf16[128,1024]{1,0:T(8,128)(2,1)S(1)} %collective-permute-done.23.refs_0_, bf16[4096,2048]{1,0:T(8,128)(2,1)} %get-tuple-element.124.refs_1_, f32[128,2048]{1,0:T(8,128)S(1)} %down.27.refs_2_), custom_call_target="tpu_custom_call" | custom-call | flops 8388608 | bytes 65536 | tf_op jit(solution)/shard_map/cond/branch_2_fun/down/pallas_call | solution.py:431
  69.6 3.6 %down.29 = (f32[128,2048]{1,0:T(8,128)S(1)}, bf16[1024,2048]{1,0:T(8,128)(2,1)S(1)}) custom-call(s32[1]{0:T(128)} %get-tuple-element.116.side, bf16[128,1024]{1,0:T(8,128)(2,1)S(1)} %collective-permute-done.21.refs_0_, bf16[4096,2048]{1,0:T(8,128)(2,1)} %get-tuple-element.124.refs_1_, f32[128,2048]{1,0:T(8,128)S(1)} %down.28.refs_2_), custom_call_target="tpu_custom_call" | custom-call | flops 8388608 | bytes 65536 | tf_op jit(solution)/shard_map/cond/branch_2_fun/down/pallas_call | solution.py:431
  73.2 0.3 collective-permute-done.22.a_ref
  73.5 2.8 %down_unpack.9 = (bf16[384,512]{1,0:T(8,128)(2,1)S(1)}, bf16[384,512]{1,0:T(8,128)(2,1)S(1)}) custom-call(s32[32]{0:T(128)S(1)} %get-tuple-element.115.layout, bf16[128,1024]{1,0:T(8,128)(2,1)S(1)} %collective-permute-done.22.a_ref, bf16[1024,2048]{1,0:T(8,128)(2,1)S(1)} %get-tuple-element.126.w_ref, f32[128,2048]{1,0:T(8,128)S(1)} %get-tuple-element.127.before_ref), custom_call_target="tpu_custom_call" | custom-call | flops 8388608 | bytes 16384 | tf_op jit(solution)/shard_map/cond/branch_2_fun/down_unpack/pallas_call | solution.py:488
  76.6 0.1 collective-permute-start.64
  76.6 1.7 %collective-permute-done.64 = bf16[384,512]{1,0:T(8,128)(2,1)S(1)} collective-permute-done((bf16[384,512]{1,0:T(8,128)(2,1)S(1)}, bf16[384,512]{1,0:T(8,128)(2,1)S(1)}, u32[]{:S(2)}, u32[]{:S(2)}) %collective-permute-start.64) | collective-permute-done | bytes 393248 | tf_op jit(solution)/shard_map/ppermute | solution.py:538
  78.4 1.6 %collective-permute-start.67 = (bf16[96,512]{1,0:T(8,128)(2,1)S(1)}, bf16[96,512]{1,0:T(8,128)(2,1)S(1)}, u32[]{:S(2)}, u32[]{:S(2)}) collective-permute-start(bf16[96,512]{1,0:T(8,128)(2,1)S(1)} %add_convert_fusion.1), channel_id=1, source_target_pairs={{0,2},{1,3},{2,0},{3,1},{4,6},{5,7},{6,4},{7,5},{8,10},{9,11},{10,... | collective-permute-start | bytes 294920 | tf_op jit(solution)/shard_map/ppermute | solution.py:538
  80.0 3.3 %collective-permute-done.67 = bf16[96,512]{1,0:T(8,128)(2,1)S(1)} collective-permute-done((bf16[96,512]{1,0:T(8,128)(2,1)S(1)}, bf16[96,512]{1,0:T(8,128)(2,1)S(1)}, u32[]{:S(2)}, u32[]{:S(2)}) %collective-permute-start.67) | collective-permute-done | bytes 98336 | tf_op jit(solution)/shard_map/ppermute | solution.py:538
  83.3 0.1 add_convert_fusion
  83.4 1.6 %collective-permute-start.65 = (bf16[96,512]{1,0:T(8,128)(2,1)S(1)}, bf16[96,512]{1,0:T(8,128)(2,1)S(1)}, u32[]{:S(2)}, u32[]{:S(2)}) collective-permute-start(bf16[96,512]{1,0:T(8,128)(2,1)S(1)} %get-tuple-element.237), channel_id=1, source_target_pairs={{0,2},{1,3},{2,0},{3,1},{4,6},{5,7},{6,4},{7,5},{8,10},{9,11},{10,... | collective-permute-start | bytes 294920 | tf_op jit(solution)/shard_map/ppermute | solution.py:538
  84.9 4.6 %collective-permute-start.69 = (bf16[48,512]{1,0:T(8,128)(2,1)S(1)}, bf16[48,512]{1,0:T(8,128)(2,1)S(1)}, u32[]{:S(2)}, u32[]{:S(2)}) collective-permute-start(bf16[48,512]{1,0:T(8,128)(2,1)S(1)} %get-tuple-element.240), channel_id=1, source_target_pairs={{0,12},{4,8},{8,4},{12,0},{1,13},{5,9},{9,5},{13,1},{2,14},{6,10},... | collective-permute-start | bytes 147464 | tf_op jit(solution)/shard_map/ppermute | solution.py:538
  89.6 0.7 collective-permute-start.66
  90.3 1.4 %collective-permute-done.69.refs_9_ = bf16[48,512]{1,0:T(8,128)(2,1)S(1)} collective-permute-done((bf16[48,512]{1,0:T(8,128)(2,1)S(1)}, bf16[48,512]{1,0:T(8,128)(2,1)S(1)}, u32[]{:S(2)}, u32[]{:S(2)}) %collective-permute-start.69) | collective-permute-done | bytes 49184 | tf_op jit(solution)/shard_map/ppermute | solution.py:538
  91.7 2.8 %collective-permute-done.68.refs_8_ = bf16[48,512]{1,0:T(8,128)(2,1)S(1)} collective-permute-done((bf16[48,512]{1,0:T(8,128)(2,1)S(1)}, bf16[48,512]{1,0:T(8,128)(2,1)S(1)}, u32[]{:S(2)}, u32[]{:S(2)}) %collective-permute-start.68) | collective-permute-done | bytes 49184 | tf_op jit(solution)/shard_map/ppermute | solution.py:538
  94.6 1.6 %finish.1 = bf16[15,8192]{1,0:T(8,128)(2,1)} custom-call(s32[15]{0:T(128)} %lengths.5, s32[1]{0:T(128)} %bitcast.49.side, f32[15,2048]{1,0:T(8,128)S(1)} %get-tuple-element.206.refs_0_, f32[15,2048]{1,0:T(8,128)S(1)} %get-tuple-element.207.refs_1_, f32[15,2048]{1,0:T(8,128)S(1)} %get-tuple-element.208.refs_2_, f32[15,2048]{1,0:T(8,128)S(1)} %get-tuple-element.209.refs_3_, ...), custom_call_target="tpu_custom_call" | custom-call | flops 61440 | bytes 15360 | tf_op jit(solution)/shard_map/finish/pallas_call | solution.py:526
  (23 shorter events, 0.3 us)
Async XLA Ops:
  5.6 10.4 %collective-permute-start.56 = (bf16[32,2048]{1,0:T(8,128)(2,1)S(1)}, bf16[32,2048]{1,0:T(8,128)(2,1)S(1)}, u32[]{:S(2)}, u32[]{:S(2)}) collective-permute-start(bf16[32,2048]{1,0:T(8,128)(2,1)S(1)} %pad_maximum_fusion.7), channel_id=1, source_target_pairs={{0,8},{4,12},{8,0},{12,4},{1,9},{5,13},{9,1},{13,5},{2,10},{6,14},... | collective-permute-start | bytes 393224 | tf_op jit(solution)/shard_map/ppermute | solution.py:538
  16.1 5.0 %collective-permute-start.57 = (bf16[32,2048]{1,0:T(8,128)(2,1)S(1)}, bf16[32,2048]{1,0:T(8,128)(2,1)S(1)}, u32[]{:S(2)}, u32[]{:S(2)}) collective-permute-start(bf16[32,2048]{1,0:T(8,128)(2,1)S(1)} %pad_maximum_fusion.9), channel_id=1, source_target_pairs={{0,4},{4,0},{8,12},{12,8},{1,5},{5,1},{9,13},{13,9},{2,6},{6,2},{1... | collective-permute-start | bytes 393224 | tf_op jit(solution)/shard_map/ppermute | solution.py:538
  16.9 6.3 %collective-permute-start.60 = (bf16[32,2048]{1,0:T(8,128)(2,1)S(1)}, bf16[32,2048]{1,0:T(8,128)(2,1)S(1)}, u32[]{:S(2)}, u32[]{:S(2)}) collective-permute-start(bf16[32,2048]{1,0:T(8,128)(2,1)S(1)} %pad_maximum_fusion.8.refs_0_), channel_id=1, source_target_pairs={{0,2},{1,3},{2,0},{3,1},{4,6},{5,7},{6,4},{7,5},{8,10},{9,11},{10,... | collective-permute-start | bytes 393224 | tf_op jit(solution)/shard_map/ppermute | solution.py:538
  21.1 5.0 %collective-permute-start.61 = (bf16[32,2048]{1,0:T(8,128)(2,1)S(1)}, bf16[32,2048]{1,0:T(8,128)(2,1)S(1)}, u32[]{:S(2)}, u32[]{:S(2)}) collective-permute-start(bf16[32,2048]{1,0:T(8,128)(2,1)S(1)} %collective-permute-done.57.refs_1_), channel_id=1, source_target_pairs={{0,2},{1,3},{2,0},{3,1},{4,6},{5,7},{6,4},{7,5},{8,10},{9,11},{10,... | collective-permute-start | bytes 393224 | tf_op jit(solution)/shard_map/ppermute | solution.py:538
  22.6 3.5 %collective-permute-start.58 = (bf16[32,2048]{1,0:T(8,128)(2,1)S(1)}, bf16[32,2048]{1,0:T(8,128)(2,1)S(1)}, u32[]{:S(2)}, u32[]{:S(2)}) collective-permute-start(bf16[32,2048]{1,0:T(8,128)(2,1)S(1)} %pad_maximum_fusion.8.refs_0_), channel_id=1, source_target_pairs={{0,1},{1,0},{2,3},{3,2},{4,5},{5,4},{6,7},{7,6},{8,9},{9,8},{10,11... | collective-permute-start | bytes 393224 | tf_op jit(solution)/shard_map/ppermute | solution.py:538
  22.6 3.5 %collective-permute-start.59 = (bf16[32,2048]{1,0:T(8,128)(2,1)S(1)}, bf16[32,2048]{1,0:T(8,128)(2,1)S(1)}, u32[]{:S(2)}, u32[]{:S(2)}) collective-permute-start(bf16[32,2048]{1,0:T(8,128)(2,1)S(1)} %collective-permute-done.57.refs_1_), channel_id=1, source_target_pairs={{0,1},{1,0},{2,3},{3,2},{4,5},{5,4},{6,7},{7,6},{8,9},{9,8},{10,11... | collective-permute-start | bytes 393224 | tf_op jit(solution)/shard_map/ppermute | solution.py:538
  23.1 3.0 %collective-permute-start.62 = (bf16[32,2048]{1,0:T(8,128)(2,1)S(1)}, bf16[32,2048]{1,0:T(8,128)(2,1)S(1)}, u32[]{:S(2)}, u32[]{:S(2)}) collective-permute-start(bf16[32,2048]{1,0:T(8,128)(2,1)S(1)} %collective-permute-done.60.refs_4_), channel_id=1, source_target_pairs={{0,1},{1,0},{2,3},{3,2},{4,5},{5,4},{6,7},{7,6},{8,9},{9,8},{10,11... | collective-permute-start | bytes 393224 | tf_op jit(solution)/shard_map/ppermute | solution.py:538
  26.1 1.3 %collective-permute-start.63 = (bf16[32,2048]{1,0:T(8,128)(2,1)S(1)}, bf16[32,2048]{1,0:T(8,128)(2,1)S(1)}, u32[]{:S(2)}, u32[]{:S(2)}) collective-permute-start(bf16[32,2048]{1,0:T(8,128)(2,1)S(1)} %collective-permute-done.61.refs_5_), channel_id=1, source_target_pairs={{0,1},{1,0},{2,3},{3,2},{4,5},{5,4},{6,7},{7,6},{8,9},{9,8},{10,11... | collective-permute-start | bytes 393224 | tf_op jit(solution)/shard_map/ppermute | solution.py:538
  31.1 5.6 %collective-permute-start.17 = (bf16[128,512]{1,0:T(8,128)(2,1)S(1)}, bf16[128,512]{1,0:T(8,128)(2,1)S(1)}, u32[]{:S(2)}, u32[]{:S(2)}) collective-permute-start(bf16[128,512]{1,0:T(8,128)(2,1)S(1)} %slice.157), channel_id=1, source_target_pairs={{0,4},{4,0},{8,12},{12,8},{1,5},{5,1},{9,13},{13,9},{2,6},{6,2},{1... | collective-permute-start | bytes 393224 | tf_op jit(solution)/shard_map/cond/branch_2_fun/ppermute | solution.py:538
  35.6 8.1 %collective-permute-start.16 = (bf16[128,512]{1,0:T(8,128)(2,1)S(1)}, bf16[128,512]{1,0:T(8,128)(2,1)S(1)}, u32[]{:S(2)}, u32[]{:S(2)}) collective-permute-start(bf16[128,512]{1,0:T(8,128)(2,1)S(1)} %slice_bitcast_fusion.7), channel_id=1, source_target_pairs={{0,4},{4,0},{8,12},{12,8},{1,5},{5,1},{9,13},{13,9},{2,6},{6,2},{1... | collective-permute-start | bytes 393224 | tf_op jit(solution)/shard_map/cond/branch_2_fun/ppermute | solution.py:538
  36.7 11.4 %collective-permute-start.19 = (bf16[128,512]{1,0:T(8,128)(2,1)S(1)}, bf16[128,512]{1,0:T(8,128)(2,1)S(1)}, u32[]{:S(2)}, u32[]{:S(2)}) collective-permute-start(bf16[128,512]{1,0:T(8,128)(2,1)S(1)} %fusion.16), channel_id=1, source_target_pairs={{0,8},{4,12},{8,0},{12,4},{1,9},{5,13},{9,1},{13,5},{2,10},{6,14},... | collective-permute-start | bytes 393224 | tf_op jit(solution)/shard_map/cond/branch_2_fun/ppermute | solution.py:538
  43.7 8.8 %collective-permute-start.18 = (bf16[2,128,512]{2,1,0:T(8,128)(2,1)S(1)}, bf16[2,128,512]{2,1,0:T(8,128)(2,1)S(1)}, u32[]{:S(2)}, u32[]{:S(2)}) collective-permute-start(bf16[2,128,512]{2,1,0:T(8,128)(2,1)S(1)} %up.28), channel_id=1, source_target_pairs={{0,4},{4,0},{8,12},{12,8},{1,5},{5,1},{9,13},{13,9},{2,6},{6,2},{1... | collective-permute-start | bytes 786440 | tf_op jit(solution)/shard_map/cond/branch_2_fun/ppermute | solution.py:538
  44.0 7.6 %collective-permute-start.20 = (bf16[128,512]{1,0:T(8,128)(2,1)S(1)}, bf16[128,512]{1,0:T(8,128)(2,1)S(1)}, u32[]{:S(2)}, u32[]{:S(2)}) collective-permute-start(bf16[128,512]{1,0:T(8,128)(2,1)S(1)} %fusion.17), channel_id=1, source_target_pairs={{0,8},{4,12},{8,0},{12,4},{1,9},{5,13},{9,1},{13,5},{2,10},{6,14},... | collective-permute-start | bytes 393224 | tf_op jit(solution)/shard_map/cond/branch_2_fun/ppermute | solution.py:538
  52.6 13.7 %collective-permute-start.21 = (bf16[128,1024]{1,0:T(8,128)(2,1)S(1)}, bf16[128,1024]{1,0:T(8,128)(2,1)S(1)}, u32[]{:S(2)}, u32[]{:S(2)}) collective-permute-start(bf16[128,1024]{1,0:T(8,128)(2,1)S(1)} %pad_maximum_fusion.2.refs_0_), channel_id=1, source_target_pairs={{0,8},{4,12},{8,0},{12,4},{1,9},{5,13},{9,1},{13,5},{2,10},{6,14},... | collective-permute-start | bytes 786440 | tf_op jit(solution)/shard_map/cond/branch_2_fun/ppermute | solution.py:538
  55.3 11.8 %collective-permute-start.23 = (bf16[128,1024]{1,0:T(8,128)(2,1)S(1)}, bf16[128,1024]{1,0:T(8,128)(2,1)S(1)}, u32[]{:S(2)}, u32[]{:S(2)}) collective-permute-start(bf16[128,1024]{1,0:T(8,128)(2,1)S(1)} %pad_maximum_fusion.2.refs_0_), channel_id=1, source_target_pairs={{0,4},{4,0},{8,12},{12,8},{1,5},{5,1},{9,13},{13,9},{2,6},{6,2},{1... | collective-permute-start | bytes 786440 | tf_op jit(solution)/shard_map/cond/branch_2_fun/ppermute | solution.py:538
  66.4 7.1 %collective-permute-start.22 = (bf16[128,1024]{1,0:T(8,128)(2,1)S(1)}, bf16[128,1024]{1,0:T(8,128)(2,1)S(1)}, u32[]{:S(2)}, u32[]{:S(2)}) collective-permute-start(bf16[128,1024]{1,0:T(8,128)(2,1)S(1)} %collective-permute-done.21.refs_0_), channel_id=1, source_target_pairs={{0,4},{4,0},{8,12},{12,8},{1,5},{5,1},{9,13},{13,9},{2,6},{6,2},{1... | collective-permute-start | bytes 786440 | tf_op jit(solution)/shard_map/cond/branch_2_fun/ppermute | solution.py:538
  76.6 1.8 %collective-permute-start.64 = (bf16[384,512]{1,0:T(8,128)(2,1)S(1)}, bf16[384,512]{1,0:T(8,128)(2,1)S(1)}, u32[]{:S(2)}, u32[]{:S(2)}) collective-permute-start(bf16[384,512]{1,0:T(8,128)(2,1)S(1)} %get-tuple-element.221), channel_id=1, source_target_pairs={{0,1},{1,0},{2,3},{3,2},{4,5},{5,4},{6,7},{7,6},{8,9},{9,8},{10,11... | collective-permute-start | bytes 1179656 | tf_op jit(solution)/shard_map/ppermute | solution.py:538
  78.4 4.9 %collective-permute-start.67 = (bf16[96,512]{1,0:T(8,128)(2,1)S(1)}, bf16[96,512]{1,0:T(8,128)(2,1)S(1)}, u32[]{:S(2)}, u32[]{:S(2)}) collective-permute-start(bf16[96,512]{1,0:T(8,128)(2,1)S(1)} %add_convert_fusion.1), channel_id=1, source_target_pairs={{0,2},{1,3},{2,0},{3,1},{4,6},{5,7},{6,4},{7,5},{8,10},{9,11},{10,... | collective-permute-start | bytes 294920 | tf_op jit(solution)/shard_map/ppermute | solution.py:538
  83.4 6.2 %collective-permute-start.65 = (bf16[96,512]{1,0:T(8,128)(2,1)S(1)}, bf16[96,512]{1,0:T(8,128)(2,1)S(1)}, u32[]{:S(2)}, u32[]{:S(2)}) collective-permute-start(bf16[96,512]{1,0:T(8,128)(2,1)S(1)} %get-tuple-element.237), channel_id=1, source_target_pairs={{0,2},{1,3},{2,0},{3,1},{4,6},{5,7},{6,4},{7,5},{8,10},{9,11},{10,... | collective-permute-start | bytes 294920 | tf_op jit(solution)/shard_map/ppermute | solution.py:538
  84.9 6.8 %collective-permute-start.69 = (bf16[48,512]{1,0:T(8,128)(2,1)S(1)}, bf16[48,512]{1,0:T(8,128)(2,1)S(1)}, u32[]{:S(2)}, u32[]{:S(2)}) collective-permute-start(bf16[48,512]{1,0:T(8,128)(2,1)S(1)} %get-tuple-element.240), channel_id=1, source_target_pairs={{0,12},{4,8},{8,4},{12,0},{1,13},{5,9},{9,5},{13,1},{2,14},{6,10},... | collective-permute-start | bytes 147464 | tf_op jit(solution)/shard_map/ppermute | solution.py:538
  89.6 5.0 %collective-permute-start.68 = (bf16[48,512]{1,0:T(8,128)(2,1)S(1)}, bf16[48,512]{1,0:T(8,128)(2,1)S(1)}, u32[]{:S(2)}, u32[]{:S(2)}) collective-permute-start(bf16[48,512]{1,0:T(8,128)(2,1)S(1)} %get-tuple-element.241), channel_id=1, source_target_pairs={{0,8},{4,12},{8,0},{12,4},{1,9},{5,13},{9,1},{13,5},{2,10},{6,14},... | collective-permute-start | bytes 147464 | tf_op jit(solution)/shard_map/ppermute | solution.py:538
  89.6 4.9 %collective-permute-start.66 = (bf16[48,512]{1,0:T(8,128)(2,1)S(1)}, bf16[48,512]{1,0:T(8,128)(2,1)S(1)}, u32[]{:S(2)}, u32[]{:S(2)}) collective-permute-start(bf16[48,512]{1,0:T(8,128)(2,1)S(1)} %get-tuple-element.242), channel_id=1, source_target_pairs={{0,4},{4,0},{8,12},{12,8},{1,5},{5,1},{9,13},{13,9},{2,6},{6,2},{1... | collective-permute-start | bytes 147464 | tf_op jit(solution)/shard_map/ppermute | solution.py:538
where the time goes:
time: 97.4 us; the launch traced here: 96.2 us
  Pallas kernels  34.7 us (36%)
  waiting for transfers between devices  30.5 us (31%)
  starting transfers between devices  29.4 us (30%)
    ppermute x22, waiting for transfers between devices, swap(): return lax.ppermute(x, axis, [(j, j ^ mask) for j in range(count)])  30.5 us
    ppermute x22, starting transfers between devices, swap(): return lax.ppermute(x, axis, [(j, j ^ mask) for j in range(count)])  29.4 us
    pallas_call x2, Pallas kernels, attend(): pl.pallas_call(functools.partial(attend_kernel, masks=masks, sides=sides,...  10.3 us
    pallas_call x3, Pallas kernels, down(): pl.pallas_call(functools.partial(down_kernel, first=before is None, mask=...  8.67 us
    pallas_call x3, Pallas kernels, up(): pl.pallas_call(functools.partial(up_kernel, masks=masks), in_specs=[smem,...  8.38 us
    pallas_call x1, Pallas kernels, pack_up(): pl.pallas_call(functools.partial(pack_up_kernel, mask=mask, limits=limits...  2.83 us
    pallas_call x1, Pallas kernels, down_unpack(): pl.pallas_call(down_unpack_kernel, in_specs=[smem, vmem, vmem, vmem], out...  2.82 us
  transfers between devices with their start and end apart: 22, of which 14 were waited for; matrix products, arithmetic and copies ran while one was open for 0% of the time, Pallas kernels for 23%

commit v1 on v0

--- a/solution.py
+++ b/solution.py
@@ -13,6 +13,8 @@
 GROUP = 8
 LIVE_CAP = 12
 PAD = 16
+TALL = 2 * LIVE_CAP
+EMPTY = 1e30
 
 epsilon = 1e-05
 bf16, f32, i32 = jnp.bfloat16, jnp.float32, jnp.int32
@@ -139,7 +141,9 @@
         copy.wait()
     values_to_come = brought[1]
 
-    pick, count = live_pick(lengths, slots, PAD, 0, False)
+    picks = [live_pick(lengths, slots, TALL, head * LIVE_CAP, False) for head in range(heads)]
+    rank = lax.broadcasted_iota(i32, (TALL, HEAD), 0)
+    empty = jnp.where(rank < LIVE_CAP, rank, rank - LIVE_CAP) >= picks[0][1]
     squares = jnp.zeros((slots, HEAD), f32)
     bias = bias_ref[...][None]
     jobs = [(n, head) for n in range(len(masks)) for head in range(heads)]
@@ -191,9 +195,11 @@
             squares = squares + mixed * mixed
             gain = gain_ref[pl.ds(block * (step // HEAD) + job[1] * GROUP + g, 1), :]
             gained = pad_rows((mixed * gain).astype(bf16))
-            rows = jnp.dot(pick, gained, preferred_element_type=f32)
-            counted = lax.broadcasted_iota(i32, rows.shape, 0) == PAD - 1
-            sends[job[0]][:, at] = jnp.where(counted, count.astype(f32), rows).astype(bf16)
+            rows = jnp.dot(picks[job[1]][0], gained, preferred_element_type=f32)
+            to = slice(g * HEAD, (g + 1) * HEAD)
+            if job[1]:
+                rows = jnp.where(empty, EMPTY, rows + sends[job[0]][:, to].astype(f32))
+            sends[job[0]][:, to] = rows.astype(bf16)
     square_ref[...] = squares
 
 
@@ -205,7 +211,7 @@
     first = before is None
     vmem, anywhere = pl.BlockSpec(memory_space=pltpu.VMEM), pl.BlockSpec(memory_space=pl.ANY)
     smem = pl.BlockSpec(memory_space=pltpu.SMEM)
-    out_shape = [jax.ShapeDtypeStruct((PAD, step), bf16)] * len(masks)
+    out_shape = [jax.ShapeDtypeStruct((TALL, step // 2), bf16)] * len(masks)
     out_shape += [jax.ShapeDtypeStruct((slots, step), f32)] * len(masks)
     out_shape += [jax.ShapeDtypeStruct((slots, HEAD), f32)]
     if first:
@@ -297,12 +303,15 @@
 
 
 def find_layout(side, shard, gathered, layout, step_ref, limits):
-    pieces = gathered[0].shape[0] // PAD
+    pieces = gathered[0].shape[0] // TALL
     devices = len(gathered) * pieces
     counts, places = [None] * devices, [None] * devices
+    number = lax.broadcasted_iota(i32, (LIVE_CAP, HEAD), 0) + 1
     for part in range(len(gathered)):
+        marks = gathered[part][:, :HEAD].astype(f32)
         for piece, mask in enumerate(PIECES[part % 2]):
-            last = gathered[part][piece * PAD : (piece + 1) * PAD, :HEAD].astype(f32)[PAD - 1 :]
+            rows = marks[piece * TALL : piece * TALL + LIVE_CAP]
+            last = jnp.where(rows < EMPTY / 2, number, 0).astype(f32)
             place = part // 2 * 4 + mask
             counts[place] = jnp.max(last).astype(i32)
             places[place] = (side[0] ^ mask) * 4 + (shard[0] ^ (part // 2))
@@ -334,26 +343,28 @@
     find_layout(side, shard, gathered, layout, step_ref, limits)
     rows, depth = packed_ref.shape
     per = gathered[0].shape[0]
-    lane = lax.broadcasted_iota(i32, (rows, per), 1)
-    row = lax.broadcasted_iota(i32, (rows, per), 0)
-    devices = len(gathered) * (per // PAD)
-    picks = []
-    for part in range(len(gathered)):
-        target = jnp.full((rows, per), -1, i32)
-        for piece, mask in enumerate(PIECES[part % 2]):
-            place = part // 2 * 4 + mask
-            base, count = layout[place], layout[devices + place]
-            inside = lane - piece * PAD
-            mine = jnp.logical_and(inside >= 0, inside < count)
-            target = jnp.where(mine, base + inside, target)
-        picks.append((target == row).astype(f32).astype(bf16))
-    pick = jnp.concatenate(picks, axis=1)
-
-    @pl.loop(0, depth // DOWN_TILE)
-    def _(t):
-        at = pl.ds(pl.multiple_of(t * DOWN_TILE, DOWN_TILE), DOWN_TILE)
-        pieces = jnp.concatenate([part[:, at] for part in gathered], axis=0)
-        packed_ref[:, at] = jnp.dot(pick, pieces, preferred_element_type=f32).astype(bf16)
+    pieces = per // TALL
+    devices = len(gathered) * pieces
+    shape = (8, len(gathered) * per)
+    lane = lax.broadcasted_iota(i32, shape, 1)
+    row = lax.broadcasted_iota(i32, (rows, shape[1]), 0)
+    for half in range(2):
+        target = jnp.full(shape, -1, i32)
+        for part in range(len(gathered)):
+            for piece, other in enumerate(PIECES[part % 2]):
+                place = part // 2 * 4 + other
+                base, count = layout[place], layout[devices + place]
+                inside = lane - (part * per + piece * TALL + half * LIVE_CAP)
+                mine = jnp.logical_and(inside >= 0, inside < count)
+                target = jnp.where(mine, base + inside, target)
+        pick = (target[:1] == row).astype(f32).astype(bf16)
+
+        @pl.loop(0, depth // 2 // DOWN_TILE)
+        def _(t):
+            at = pl.ds(pl.multiple_of(t * DOWN_TILE, DOWN_TILE), DOWN_TILE)
+            to = pl.ds(pl.multiple_of(half * (depth // 2) + t * DOWN_TILE, DOWN_TILE), DOWN_TILE)
+            found = jnp.concatenate([part[:, at] for part in gathered], axis=0)
+            packed_ref[:, to] = jnp.dot(pick, found, preferred_element_type=f32).astype(bf16)
 
     @pl.loop(0, width // UP_TILE)
     def _(t):
@@ -366,7 +377,7 @@
 
 def pack_up(side, shard, gathered, w_up, rows, width, mask, limits):
     depth = w_up.shape[0]
-    devices = len(gathered) * gathered[0].shape[0] // PAD
+    devices = len(gathered) * gathered[0].shape[0] // TALL
     vmem, smem = pl.BlockSpec(memory_space=pltpu.VMEM), pl.BlockSpec(memory_space=pltpu.SMEM)
     return pl.pallas_call(
         functools.partial(pack_up_kernel, mask=mask, limits=limits),
@@ -593,8 +604,8 @@
     (to_2, to_3), mixed_far, squares_far, copies = attend(inputs, side, 4, (2, 3), None)
     met = swap(jnp.concatenate([to_2, to_3], axis=0), "side", 4, 2)
     (own, to_1), mixed_near, squares_near, _ = attend(inputs, side, 4, (0, 1), copies)
-    first = jnp.concatenate([own, met[:PAD]], axis=0)
-    second = swap(jnp.concatenate([to_1, met[PAD:]], axis=0), "side", 4, 1)
+    first = jnp.concatenate([own, met[:TALL]], axis=0)
+    second = swap(jnp.concatenate([to_1, met[TALL:]], axis=0), "side", 4, 1)
     gathered = []
     by_x = [swap(here, "shard", 4, 2) for here in (first, second)]
     by_core = [swap(here, "shard", 4, 1) for here in (first, second)]

time: 97.4 us -> 95.8 us (0.984); the launches traced: 96.2 us -> 97.5 us
  waiting for transfers between devices: 30.5 us -> 37.3 us
  starting transfers between devices: 29.4 us -> 23.9 us
    ppermute x22, waiting for transfers between devices: 30.5 us -> 37.3 us  [swap(): return lax.ppermute(x, axis, [(j, j ^ mask) for j in range(count)])]
    ppermute x22, starting transfers between devices: 29.4 us -> 23.9 us  [swap(): return lax.ppermute(x, axis, [(j, j ^ mask) for j in range(count)])]
  transfers between devices with their start and end apart: 22 -> 22, of which waited for: 14 -> 17; matrix products, arithmetic and copies ran while one was open for 0% -> 0% of each run, Pallas kernels for 23% -> 23%
where the time goes in v1:
time: 95.8 us; the launch traced here: 97.5 us
  waiting for transfers between devices  37.3 us (39%)
  Pallas kernels  34.8 us (36%)
  starting transfers between devices  23.9 us (25%)
    ppermute x22, waiting for transfers between devices, swap(): return lax.ppermute(x, axis, [(j, j ^ mask) for j in range(count)])  37.3 us
    ppermute x22, starting transfers between devices, swap(): return lax.ppermute(x, axis, [(j, j ^ mask) for j in range(count)])  23.9 us
    pallas_call x2, Pallas kernels, attend(): pl.pallas_call(functools.partial(attend_kernel, masks=masks, sides=sides,...  10.4 us
    pallas_call x3, Pallas kernels, down(): pl.pallas_call(functools.partial(down_kernel, first=before is None, mask=...  8.81 us
    pallas_call x3, Pallas kernels, up(): pl.pallas_call(functools.partial(up_kernel, masks=masks), in_specs=[smem,...  8.44 us
    pallas_call x1, Pallas kernels, down_unpack(): pl.pallas_call(down_unpack_kernel, in_specs=[smem, vmem, vmem, vmem], out...  2.91 us
    pallas_call x1, Pallas kernels, pack_up(): pl.pallas_call(functools.partial(pack_up_kernel, mask=mask, limits=limits...  2.64 us
  transfers between devices with their start and end apart: 22, of which 17 were waited for; matrix products, arithmetic and copies ran while one was open for 0% of the time, Pallas kernels for 23%

profile of v1, /device:TPU:0, one launch (start us, length us, event | category | flops | bytes accessed | tf_op | source)
XLA Modules:
  0.0 97.5 jit_solution(4758482679632582655)
XLA Ops:
  0.0 5.6 %attend.2 = (bf16[24,1024]{1,0:T(8,128)(2,1)S(1)}, bf16[24,1024]{1,0:T(8,128)(2,1)S(1)}, f32[15,2048]{1,0:T(8,128)S(1)}, f32[15,2048]{1,0:T(8,128)S(1)}, f32[15,...) custom-call(s32[15]{0:T(128)} %lengths.5, ...), custom_call_target="tpu_custom_call" | custom-call | flops 31250000 | bytes 57344 | tf_op jit(solution)/shard_map/attend/pallas_call | solution.py:236
  5.6 4.1 %collective-permute-start.56 = (bf16[48,1024]{1,0:T(8,128)(2,1)S(1)}, bf16[48,1024]{1,0:T(8,128)(2,1)S(1)}, u32[]{:S(2)}, u32[]{:S(2)}) collective-permute-start(bf16[48,1024]{1,0:T(8,128)(2,1)S(1)} %pad_maximum_fusion.7), channel_id=1, source_target_pairs={{0,8},{4,12},{8,0},{12,4},{1,9},{5,13},{9,1},{13,5},{2,10},{6,14},... | collective-permute-start | bytes 294920 | tf_op jit(solution)/shard_map/ppermute | solution.py:549
  9.8 4.8 %attend.3 = (bf16[24,1024]{1,0:T(8,128)(2,1)S(1)}, bf16[24,1024]{1,0:T(8,128)(2,1)S(1)}, f32[15,2048]{1,0:T(8,128)S(1)}, f32[15,2048]{1,0:T(8,128)S(1)}, f32[15,128]{1,0:T(8,128)S(1)}) custom-call(s32[15]{0:T(128)} %lengths.5, s32[1]{0:T(128)} %bitcast.49.side, bf16[15,8192]{1,0:T(8,128)(2,1)S(1)} %get-tuple-element.201.refs_0_, ...), custom_call_target="tpu_custom_call" | custom-call | flops 31250000 | bytes 57344 | tf_op jit(solution)/shard_map/attend/pallas_call | solution.py:236
  14.5 0.1 collective-permute-done.56
  14.7 1.5 %collective-permute-start.57 = (bf16[48,1024]{1,0:T(8,128)(2,1)S(1)}, bf16[48,1024]{1,0:T(8,128)(2,1)S(1)}, u32[]{:S(2)}, u32[]{:S(2)}) collective-permute-start(bf16[48,1024]{1,0:T(8,128)(2,1)S(1)} %pad_maximum_fusion.9), channel_id=1, source_target_pairs={{0,4},{4,0},{8,12},{12,8},{1,5},{5,1},{9,13},{13,9},{2,6},{6,2},{1... | collective-permute-start | bytes 294920 | tf_op jit(solution)/shard_map/ppermute | solution.py:549
  16.2 1.5 %collective-permute-start.60 = (bf16[48,1024]{1,0:T(8,128)(2,1)S(1)}, bf16[48,1024]{1,0:T(8,128)(2,1)S(1)}, u32[]{:S(2)}, u32[]{:S(2)}) collective-permute-start(bf16[48,1024]{1,0:T(8,128)(2,1)S(1)} %pad_maximum_fusion.8.refs_0_), channel_id=1, source_target_pairs={{0,2},{1,3},{2,0},{3,1},{4,6},{5,7},{6,4},{7,5},{8,10},{9,11},{10,... | collective-permute-start | bytes 294920 | tf_op jit(solution)/shard_map/ppermute | solution.py:549
  17.8 1.6 %collective-permute-done.57.refs_1_ = bf16[48,1024]{1,0:T(8,128)(2,1)S(1)} collective-permute-done((bf16[48,1024]{1,0:T(8,128)(2,1)S(1)}, bf16[48,1024]{1,0:T(8,128)(2,1)S(1)}, u32[]{:S(2)}, u32[]{:S(2)}) %collective-permute-start.57) | collective-permute-done | bytes 98336 | tf_op jit(solution)/shard_map/ppermute | solution.py:549
  19.4 1.5 %collective-permute-start.61 = (bf16[48,1024]{1,0:T(8,128)(2,1)S(1)}, bf16[48,1024]{1,0:T(8,128)(2,1)S(1)}, u32[]{:S(2)}, u32[]{:S(2)}) collective-permute-start(bf16[48,1024]{1,0:T(8,128)(2,1)S(1)} %collective-permute-done.57.refs_1_), channel_id=1, source_target_pairs={{0,2},{1,3},{2,0},{3,1},{4,6},{5,7},{6,4},{7,5},{8,10},{9,11},{10,... | collective-permute-start | bytes 294920 | tf_op jit(solution)/shard_map/ppermute | solution.py:549
  20.9 0.0 collective-permute-start.58
  20.9 0.5 collective-permute-start.59
  21.4 0.2 collective-permute-done.60.refs_4_
  21.6 2.4 %collective-permute-done.61.refs_5_ = bf16[48,1024]{1,0:T(8,128)(2,1)S(1)} collective-permute-done((bf16[48,1024]{1,0:T(8,128)(2,1)S(1)}, bf16[48,1024]{1,0:T(8,128)(2,1)S(1)}, u32[]{:S(2)}, u32[]{:S(2)}) %collective-permute-start.61) | collective-permute-done | bytes 98336 | tf_op jit(solution)/shard_map/ppermute | solution.py:549
  24.0 1.3 %collective-permute-done.63.refs_7_ = bf16[48,1024]{1,0:T(8,128)(2,1)S(1)} collective-permute-done((bf16[48,1024]{1,0:T(8,128)(2,1)S(1)}, bf16[48,1024]{1,0:T(8,128)(2,1)S(1)}, u32[]{:S(2)}, u32[]{:S(2)}) %collective-permute-start.63) | collective-permute-done | bytes 98336 | tf_op jit(solution)/shard_map/ppermute | solution.py:549
  25.3 2.6 %pack_up.1 = (bf16[192,2048]{1,0:T(8,128)(2,1)S(1)}, bf16[192,512]{1,0:T(8,128)(2,1)S(1)}, s32[32]{0:T(128)S(1)}, s32[1]{0:T(128)}) custom-call(s32[1]{0:T(128)} %bitcast.49.side, s32[1]{0:T(128)} %bitcast.51.shard, bf16[48,1024]{1,0:T(8,128)(2,1)S(1)} %pad_maximum_fusion.8.refs_0_, bf16[48,1024]{1,0:T(8,128)(2,1)S(1)} %collective-permute-done.57.refs_1_, ...), custom_call_target="tpu_custom_call" | custom-call | flops 6291456 | bytes 32768 | tf_op jit(solution)/shard_map/pack_up/pallas_call | solution.py:382
  28.5 51.2 %conditional.1 = ((bf16[384,512]{1,0:T(8,128)(2,1)S(1)}, bf16[384,512]{1,0:T(8,128)(2,1)S(1)})) conditional(s32[]{:T(128)} %bitcast.52, (s32[1]{0:T(128)}, bf16[192,2048]{1,0:T(8,128)(2,1)S(1)}, bf16[2048,4096]{1,0:T(8,128)(2,1)}, bf16[192,512]{1,0:T(8,128)(2,1)S(1)}, bf16[4096,2048]{1,0:T(8,128)(2,1)}, ...), branch_computations={%region_0.0_spmd, %region_1.0_spmd, %region_2.0_spmd, %region_3.0_... | conditional | flops 72351744 | bytes 13820232 | solution.py:617
  28.8 1.5 %collective-permute-start.33 = (bf16[144,512]{1,0:T(8,128)(2,1)S(1)}, bf16[144,512]{1,0:T(8,128)(2,1)S(1)}, u32[]{:S(2)}, u32[]{:S(2)}) collective-permute-start(bf16[144,512]{1,0:T(8,128)(2,1)S(1)} %slice.173), channel_id=1, source_target_pairs={{0,4},{4,0},{8,12},{12,8},{1,5},{5,1},{9,13},{13,9},{2,6},{6,2},{1... | collective-permute-start | bytes 442376 | tf_op jit(solution)/shard_map/cond/branch_4_fun/ppermute | solution.py:549
  30.3 3.3 %up.33 = bf16[3,144,512]{2,1,0:T(8,128)(2,1)S(1)} custom-call(s32[1]{0:T(128)} %get-tuple-element.142.side, bf16[192,2048]{1,0:T(8,128)(2,1)S(1)} %get-tuple-element.148.x_ref, bf16[2048,4096]{1,0:T(8,128)(2,1)} %get-tuple-element.144.w_ref), custom_call_target="tpu_custom_call" | custom-call | flops 4718592 | bytes 98304 | tf_op jit(solution)/shard_map/cond/branch_4_fun/up/pallas_call | solution.py:287
  33.6 0.6 collective-permute-start.32
  34.2 0.5 collective-permute-done.33
  34.8 2.5 %collective-permute-start.35 = (bf16[144,512]{1,0:T(8,128)(2,1)S(1)}, bf16[144,512]{1,0:T(8,128)(2,1)S(1)}, u32[]{:S(2)}, u32[]{:S(2)}) collective-permute-start(bf16[144,512]{1,0:T(8,128)(2,1)S(1)} %fusion.32), channel_id=1, source_target_pairs={{0,8},{4,12},{8,0},{12,4},{1,9},{5,13},{9,1},{13,5},{2,10},{6,14},... | collective-permute-start | bytes 442376 | tf_op jit(solution)/shard_map/cond/branch_4_fun/ppermute | solution.py:549
  37.3 2.6 %up.34 = bf16[2,144,512]{2,1,0:T(8,128)(2,1)S(1)} custom-call(s32[1]{0:T(128)} %get-tuple-element.142.side, bf16[192,2048]{1,0:T(8,128)(2,1)S(1)} %get-tuple-element.148.x_ref, bf16[2048,4096]{1,0:T(8,128)(2,1)} %get-tuple-element.144.w_ref), custom_call_target="tpu_custom_call" | custom-call | flops 4718592 | bytes 65536 | tf_op jit(solution)/shard_map/cond/branch_4_fun/up/pallas_call | solution.py:287
  39.9 2.5 %collective-permute-done.32 = bf16[144,512]{1,0:T(8,128)(2,1)S(1)} collective-permute-done((bf16[144,512]{1,0:T(8,128)(2,1)S(1)}, bf16[144,512]{1,0:T(8,128)(2,1)S(1)}, u32[]{:S(2)}, u32[]{:S(2)}) %collective-permute-start.32) | collective-permute-done | bytes 147488 | tf_op jit(solution)/shard_map/cond/branch_4_fun/ppermute | solution.py:549
  42.5 0.8 collective-permute-start.36
  43.2 2.6 %up.35 = bf16[2,144,512]{2,1,0:T(8,128)(2,1)S(1)} custom-call(s32[1]{0:T(128)} %get-tuple-element.142.side, bf16[192,2048]{1,0:T(8,128)(2,1)S(1)} %get-tuple-element.148.x_ref, bf16[2048,4096]{1,0:T(8,128)(2,1)} %get-tuple-element.144.w_ref), custom_call_target="tpu_custom_call" | custom-call | flops 4718592 | bytes 65536 | tf_op jit(solution)/shard_map/cond/branch_4_fun/up/pallas_call | solution.py:287
  45.9 5.3 %collective-permute-done.36 = bf16[144,512]{1,0:T(8,128)(2,1)S(1)} collective-permute-done((bf16[144,512]{1,0:T(8,128)(2,1)S(1)}, bf16[144,512]{1,0:T(8,128)(2,1)S(1)}, u32[]{:S(2)}, u32[]{:S(2)}) %collective-permute-start.36) | collective-permute-done | bytes 147488 | tf_op jit(solution)/shard_map/cond/branch_4_fun/ppermute | solution.py:549
  51.2 2.2 %collective-permute-done.34 = bf16[2,144,512]{2,1,0:T(8,128)(2,1)S(1)} collective-permute-done((bf16[2,144,512]{2,1,0:T(8,128)(2,1)S(1)}, bf16[2,144,512]{2,1,0:T(8,128)(2,1)S(1)}, u32[]{:S(2)}, u32[]{:S(2)}) %collective-permute-start.34) | collective-permute-done | bytes 294944 | tf_op jit(solution)/shard_map/cond/branch_4_fun/ppermute | solution.py:549
  53.4 0.1 fusion.39
  53.6 1.3 %collective-permute-start.37 = (bf16[144,1024]{1,0:T(8,128)(2,1)S(1)}, bf16[144,1024]{1,0:T(8,128)(2,1)S(1)}, u32[]{:S(2)}, u32[]{:S(2)}) collective-permute-start(bf16[144,1024]{1,0:T(8,128)(2,1)S(1)} %pad_maximum_fusion.4.refs_0_), channel_id=1, source_target_pairs={{0,8},{4,12},{8,0},{12,4},{1,9},{5,13},{9,1},{13,5},{2,10},{6,14},... | collective-permute-start | bytes 884744 | tf_op jit(solution)/shard_map/cond/branch_4_fun/ppermute | solution.py:549
  54.8 1.4 %collective-permute-start.39 = (bf16[144,1024]{1,0:T(8,128)(2,1)S(1)}, bf16[144,1024]{1,0:T(8,128)(2,1)S(1)}, u32[]{:S(2)}, u32[]{:S(2)}) collective-permute-start(bf16[144,1024]{1,0:T(8,128)(2,1)S(1)} %pad_maximum_fusion.4.refs_0_), channel_id=1, source_target_pairs={{0,4},{4,0},{8,12},{12,8},{1,5},{5,1},{9,13},{13,9},{2,6},{6,2},{1... | collective-permute-start | bytes 884744 | tf_op jit(solution)/shard_map/cond/branch_4_fun/ppermute | solution.py:549
  56.3 2.6 %down.33.refs_2_ = f32[144,2048]{1,0:T(8,128)S(1)} custom-call(s32[1]{0:T(128)} %get-tuple-element.142.side, bf16[144,1024]{1,0:T(8,128)(2,1)S(1)} %pad_maximum_fusion.4.refs_0_, bf16[4096,2048]{1,0:T(8,128)(2,1)} %get-tuple-element.150.refs_1_), custom_call_target="tpu_custom_call" | custom-call | flops 9437184 | bytes 65536 | tf_op jit(solution)/shard_map/cond/branch_4_fun/down/pallas_call | solution.py:442
  58.9 9.4 %collective-permute-done.37.refs_0_ = bf16[144,1024]{1,0:T(8,128)(2,1)S(1)} collective-permute-done((bf16[144,1024]{1,0:T(8,128)(2,1)S(1)}, bf16[144,1024]{1,0:T(8,128)(2,1)S(1)}, u32[]{:S(2)}, u32[]{:S(2)}) %collective-permute-start.37) | collective-permute-done | bytes 294944 | tf_op jit(solution)/shard_map/cond/branch_4_fun/ppermute | solution.py:549
  68.3 2.6 %down.34.refs_2_ = f32[144,2048]{1,0:T(8,128)S(1)} custom-call(s32[1]{0:T(128)} %get-tuple-element.142.side, bf16[144,1024]{1,0:T(8,128)(2,1)S(1)} %collective-permute-done.39.refs_0_, bf16[4096,2048]{1,0:T(8,128)(2,1)} %get-tuple-element.150.refs_1_, f32[144,2048]{1,0:T(8,128)S(1)} %down.33.refs_2_), custom_call_target="tpu_custom_call" | custom-call | flops 9437184 | bytes 65536 | tf_op jit(solution)/shard_map/cond/branch_4_fun/down/pallas_call | solution.py:442
  70.9 3.6 %down.35 = (f32[144,2048]{1,0:T(8,128)S(1)}, bf16[1024,2048]{1,0:T(8,128)(2,1)S(1)}) custom-call(s32[1]{0:T(128)} %get-tuple-element.142.side, bf16[144,1024]{1,0:T(8,128)(2,1)S(1)} %collective-permute-done.37.refs_0_, bf16[4096,2048]{1,0:T(8,128)(2,1)} %get-tuple-element.150.refs_1_, f32[144,2048]{1,0:T(8,128)S(1)} %down.34.refs_2_), custom_call_target="tpu_custom_call" | custom-call | flops 9437184 | bytes 65536 | tf_op jit(solution)/shard_map/cond/branch_4_fun/down/pallas_call | solution.py:442
  74.5 2.2 %collective-permute-done.38.a_ref = bf16[144,1024]{1,0:T(8,128)(2,1)S(1)} collective-permute-done((bf16[144,1024]{1,0:T(8,128)(2,1)S(1)}, bf16[144,1024]{1,0:T(8,128)(2,1)S(1)}, u32[]{:S(2)}, u32[]{:S(2)}) %collective-permute-start.38) | collective-permute-done | bytes 294944 | tf_op jit(solution)/shard_map/cond/branch_4_fun/ppermute | solution.py:549
  76.8 2.9 %down_unpack.11 = (bf16[384,512]{1,0:T(8,128)(2,1)S(1)}, bf16[384,512]{1,0:T(8,128)(2,1)S(1)}) custom-call(s32[32]{0:T(128)S(1)} %get-tuple-element.141.layout, bf16[144,1024]{1,0:T(8,128)(2,1)S(1)} %collective-permute-done.38.a_ref, bf16[1024,2048]{1,0:T(8,128)(2,1)S(1)} %get-tuple-element.152.w_ref, f32[144,2048]{1,0:T(8,128)S(1)} %get-tuple-element.153.before_ref), custom_call_target="tpu_custom_call" | custom-call | flops 9437184 | bytes 18432 | tf_op jit(solution)/shard_map/cond/branch_4_fun/down_unpack/pallas_call | solution.py:499
  79.7 0.1 collective-permute-start.64
  79.8 1.7 %collective-permute-done.64 = bf16[384,512]{1,0:T(8,128)(2,1)S(1)} collective-permute-done((bf16[384,512]{1,0:T(8,128)(2,1)S(1)}, bf16[384,512]{1,0:T(8,128)(2,1)S(1)}, u32[]{:S(2)}, u32[]{:S(2)}) %collective-permute-start.64) | collective-permute-done | bytes 393248 | tf_op jit(solution)/shard_map/ppermute | solution.py:549
  81.5 1.5 %collective-permute-start.67 = (bf16[96,512]{1,0:T(8,128)(2,1)S(1)}, bf16[96,512]{1,0:T(8,128)(2,1)S(1)}, u32[]{:S(2)}, u32[]{:S(2)}) collective-permute-start(bf16[96,512]{1,0:T(8,128)(2,1)S(1)} %add_convert_fusion.1), channel_id=1, source_target_pairs={{0,2},{1,3},{2,0},{3,1},{4,6},{5,7},{6,4},{7,5},{8,10},{9,11},{10,... | collective-permute-start | bytes 294920 | tf_op jit(solution)/shard_map/ppermute | solution.py:549
  83.0 3.4 %collective-permute-done.67 = bf16[96,512]{1,0:T(8,128)(2,1)S(1)} collective-permute-done((bf16[96,512]{1,0:T(8,128)(2,1)S(1)}, bf16[96,512]{1,0:T(8,128)(2,1)S(1)}, u32[]{:S(2)}, u32[]{:S(2)}) %collective-permute-start.67) | collective-permute-done | bytes 98336 | tf_op jit(solution)/shard_map/ppermute | solution.py:549
  86.4 0.1 add_convert_fusion
  86.5 1.5 %collective-permute-start.65 = (bf16[96,512]{1,0:T(8,128)(2,1)S(1)}, bf16[96,512]{1,0:T(8,128)(2,1)S(1)}, u32[]{:S(2)}, u32[]{:S(2)}) collective-permute-start(bf16[96,512]{1,0:T(8,128)(2,1)S(1)} %get-tuple-element.237), channel_id=1, source_target_pairs={{0,2},{1,3},{2,0},{3,1},{4,6},{5,7},{6,4},{7,5},{8,10},{9,11},{10,... | collective-permute-start | bytes 294920 | tf_op jit(solution)/shard_map/ppermute | solution.py:549
  88.0 2.1 %collective-permute-start.69 = (bf16[48,512]{1,0:T(8,128)(2,1)S(1)}, bf16[48,512]{1,0:T(8,128)(2,1)S(1)}, u32[]{:S(2)}, u32[]{:S(2)}) collective-permute-start(bf16[48,512]{1,0:T(8,128)(2,1)S(1)} %get-tuple-element.238), channel_id=1, source_target_pairs={{0,12},{4,8},{8,4},{12,0},{1,13},{5,9},{9,5},{13,1},{2,14},{6,10},... | collective-permute-start | bytes 147464 | tf_op jit(solution)/shard_map/ppermute | solution.py:549
  90.1 1.1 %collective-permute-done.65 = bf16[96,512]{1,0:T(8,128)(2,1)S(1)} collective-permute-done((bf16[96,512]{1,0:T(8,128)(2,1)S(1)}, bf16[96,512]{1,0:T(8,128)(2,1)S(1)}, u32[]{:S(2)}, u32[]{:S(2)}) %collective-permute-start.65) | collective-permute-done | bytes 98336 | tf_op jit(solution)/shard_map/ppermute | solution.py:549
  91.2 1.3 %collective-permute-start.66 = (bf16[48,512]{1,0:T(8,128)(2,1)S(1)}, bf16[48,512]{1,0:T(8,128)(2,1)S(1)}, u32[]{:S(2)}, u32[]{:S(2)}) collective-permute-start(bf16[48,512]{1,0:T(8,128)(2,1)S(1)} %get-tuple-element.240), channel_id=1, source_target_pairs={{0,4},{4,0},{8,12},{12,8},{1,5},{5,1},{9,13},{13,9},{2,6},{6,2},{1... | collective-permute-start | bytes 147464 | tf_op jit(solution)/shard_map/ppermute | solution.py:549
  92.6 1.7 %collective-permute-done.69.refs_9_ = bf16[48,512]{1,0:T(8,128)(2,1)S(1)} collective-permute-done((bf16[48,512]{1,0:T(8,128)(2,1)S(1)}, bf16[48,512]{1,0:T(8,128)(2,1)S(1)}, u32[]{:S(2)}, u32[]{:S(2)}) %collective-permute-start.69) | collective-permute-done | bytes 49184 | tf_op jit(solution)/shard_map/ppermute | solution.py:549
  94.2 1.3 %collective-permute-done.68.refs_8_ = bf16[48,512]{1,0:T(8,128)(2,1)S(1)} collective-permute-done((bf16[48,512]{1,0:T(8,128)(2,1)S(1)}, bf16[48,512]{1,0:T(8,128)(2,1)S(1)}, u32[]{:S(2)}, u32[]{:S(2)}) %collective-permute-start.68) | collective-permute-done | bytes 49184 | tf_op jit(solution)/shard_map/ppermute | solution.py:549
  95.5 0.3 collective-permute-done.66.refs_7_
  95.8 1.6 %finish.1 = bf16[15,8192]{1,0:T(8,128)(2,1)} custom-call(s32[15]{0:T(128)} %lengths.5, s32[1]{0:T(128)} %bitcast.49.side, f32[15,2048]{1,0:T(8,128)S(1)} %get-tuple-element.206.refs_0_, f32[15,2048]{1,0:T(8,128)S(1)} %get-tuple-element.207.refs_1_, f32[15,2048]{1,0:T(8,128)S(1)} %get-tuple-element.208.refs_2_, f32[15,2048]{1,0:T(8,128)S(1)} %get-tuple-element.209.refs_3_, ...), custom_call_target="tpu_custom_call" | custom-call | flops 61440 | bytes 15360 | tf_op jit(solution)/shard_map/finish/pallas_call | solution.py:537
  (23 shorter events, 0.3 us)
Async XLA Ops:
  5.6 9.0 %collective-permute-start.56 = (bf16[48,1024]{1,0:T(8,128)(2,1)S(1)}, bf16[48,1024]{1,0:T(8,128)(2,1)S(1)}, u32[]{:S(2)}, u32[]{:S(2)}) collective-permute-start(bf16[48,1024]{1,0:T(8,128)(2,1)S(1)} %pad_maximum_fusion.7), channel_id=1, source_target_pairs={{0,8},{4,12},{8,0},{12,4},{1,9},{5,13},{9,1},{13,5},{2,10},{6,14},... | collective-permute-start | bytes 294920 | tf_op jit(solution)/shard_map/ppermute | solution.py:549
  14.7 4.7 %collective-permute-start.57 = (bf16[48,1024]{1,0:T(8,128)(2,1)S(1)}, bf16[48,1024]{1,0:T(8,128)(2,1)S(1)}, u32[]{:S(2)}, u32[]{:S(2)}) collective-permute-start(bf16[48,1024]{1,0:T(8,128)(2,1)S(1)} %pad_maximum_fusion.9), channel_id=1, source_target_pairs={{0,4},{4,0},{8,12},{12,8},{1,5},{5,1},{9,13},{13,9},{2,6},{6,2},{1... | collective-permute-start | bytes 294920 | tf_op jit(solution)/shard_map/ppermute | solution.py:549
  16.2 5.4 %collective-permute-start.60 = (bf16[48,1024]{1,0:T(8,128)(2,1)S(1)}, bf16[48,1024]{1,0:T(8,128)(2,1)S(1)}, u32[]{:S(2)}, u32[]{:S(2)}) collective-permute-start(bf16[48,1024]{1,0:T(8,128)(2,1)S(1)} %pad_maximum_fusion.8.refs_0_), channel_id=1, source_target_pairs={{0,2},{1,3},{2,0},{3,1},{4,6},{5,7},{6,4},{7,5},{8,10},{9,11},{10,... | collective-permute-start | bytes 294920 | tf_op jit(solution)/shard_map/ppermute | solution.py:549
  19.4 4.6 %collective-permute-start.61 = (bf16[48,1024]{1,0:T(8,128)(2,1)S(1)}, bf16[48,1024]{1,0:T(8,128)(2,1)S(1)}, u32[]{:S(2)}, u32[]{:S(2)}) collective-permute-start(bf16[48,1024]{1,0:T(8,128)(2,1)S(1)} %collective-permute-done.57.refs_1_), channel_id=1, source_target_pairs={{0,2},{1,3},{2,0},{3,1},{4,6},{5,7},{6,4},{7,5},{8,10},{9,11},{10,... | collective-permute-start | bytes 294920 | tf_op jit(solution)/shard_map/ppermute | solution.py:549
  20.9 3.1 %collective-permute-start.58 = (bf16[48,1024]{1,0:T(8,128)(2,1)S(1)}, bf16[48,1024]{1,0:T(8,128)(2,1)S(1)}, u32[]{:S(2)}, u32[]{:S(2)}) collective-permute-start(bf16[48,1024]{1,0:T(8,128)(2,1)S(1)} %pad_maximum_fusion.8.refs_0_), channel_id=1, source_target_pairs={{0,1},{1,0},{2,3},{3,2},{4,5},{5,4},{6,7},{7,6},{8,9},{9,8},{10,11... | collective-permute-start | bytes 294920 | tf_op jit(solution)/shard_map/ppermute | solution.py:549
  20.9 3.1 %collective-permute-start.59 = (bf16[48,1024]{1,0:T(8,128)(2,1)S(1)}, bf16[48,1024]{1,0:T(8,128)(2,1)S(1)}, u32[]{:S(2)}, u32[]{:S(2)}) collective-permute-start(bf16[48,1024]{1,0:T(8,128)(2,1)S(1)} %collective-permute-done.57.refs_1_), channel_id=1, source_target_pairs={{0,1},{1,0},{2,3},{3,2},{4,5},{5,4},{6,7},{7,6},{8,9},{9,8},{10,11... | collective-permute-start | bytes 294920 | tf_op jit(solution)/shard_map/ppermute | solution.py:549
  21.6 2.4 %collective-permute-start.62 = (bf16[48,1024]{1,0:T(8,128)(2,1)S(1)}, bf16[48,1024]{1,0:T(8,128)(2,1)S(1)}, u32[]{:S(2)}, u32[]{:S(2)}) collective-permute-start(bf16[48,1024]{1,0:T(8,128)(2,1)S(1)} %collective-permute-done.60.refs_4_), channel_id=1, source_target_pairs={{0,1},{1,0},{2,3},{3,2},{4,5},{5,4},{6,7},{7,6},{8,9},{9,8},{10,11... | collective-permute-start | bytes 294920 | tf_op jit(solution)/shard_map/ppermute | solution.py:549
  24.0 1.3 %collective-permute-start.63 = (bf16[48,1024]{1,0:T(8,128)(2,1)S(1)}, bf16[48,1024]{1,0:T(8,128)(2,1)S(1)}, u32[]{:S(2)}, u32[]{:S(2)}) collective-permute-start(bf16[48,1024]{1,0:T(8,128)(2,1)S(1)} %collective-permute-done.61.refs_5_), channel_id=1, source_target_pairs={{0,1},{1,0},{2,3},{3,2},{4,5},{5,4},{6,7},{7,6},{8,9},{9,8},{10,11... | collective-permute-start | bytes 294920 | tf_op jit(solution)/shard_map/ppermute | solution.py:549
  28.8 6.0 %collective-permute-start.33 = (bf16[144,512]{1,0:T(8,128)(2,1)S(1)}, bf16[144,512]{1,0:T(8,128)(2,1)S(1)}, u32[]{:S(2)}, u32[]{:S(2)}) collective-permute-start(bf16[144,512]{1,0:T(8,128)(2,1)S(1)} %slice.173), channel_id=1, source_target_pairs={{0,4},{4,0},{8,12},{12,8},{1,5},{5,1},{9,13},{13,9},{2,6},{6,2},{1... | collective-permute-start | bytes 442376 | tf_op jit(solution)/shard_map/cond/branch_4_fun/ppermute | solution.py:549
  33.6 8.8 %collective-permute-start.32 = (bf16[144,512]{1,0:T(8,128)(2,1)S(1)}, bf16[144,512]{1,0:T(8,128)(2,1)S(1)}, u32[]{:S(2)}, u32[]{:S(2)}) collective-permute-start(bf16[144,512]{1,0:T(8,128)(2,1)S(1)} %slice_bitcast_fusion.13), channel_id=1, source_target_pairs={{0,4},{4,0},{8,12},{12,8},{1,5},{5,1},{9,13},{13,9},{2,6},{6,2},{1... | collective-permute-start | bytes 442376 | tf_op jit(solution)/shard_map/cond/branch_4_fun/ppermute | solution.py:549
  34.8 11.1 %collective-permute-start.35 = (bf16[144,512]{1,0:T(8,128)(2,1)S(1)}, bf16[144,512]{1,0:T(8,128)(2,1)S(1)}, u32[]{:S(2)}, u32[]{:S(2)}) collective-permute-start(bf16[144,512]{1,0:T(8,128)(2,1)S(1)} %fusion.32), channel_id=1, source_target_pairs={{0,8},{4,12},{8,0},{12,4},{1,9},{5,13},{9,1},{13,5},{2,10},{6,14},... | collective-permute-start | bytes 442376 | tf_op jit(solution)/shard_map/cond/branch_4_fun/ppermute | solution.py:549
  42.4 11.0 %collective-permute-start.34 = (bf16[2,144,512]{2,1,0:T(8,128)(2,1)S(1)}, bf16[2,144,512]{2,1,0:T(8,128)(2,1)S(1)}, u32[]{:S(2)}, u32[]{:S(2)}) collective-permute-start(bf16[2,144,512]{2,1,0:T(8,128)(2,1)S(1)} %up.34), channel_id=1, source_target_pairs={{0,4},{4,0},{8,12},{12,8},{1,5},{5,1},{9,13},{13,9},{2,6},{6,2},{1... | collective-permute-start | bytes 884744 | tf_op jit(solution)/shard_map/cond/branch_4_fun/ppermute | solution.py:549
  42.5 8.7 %collective-permute-start.36 = (bf16[144,512]{1,0:T(8,128)(2,1)S(1)}, bf16[144,512]{1,0:T(8,128)(2,1)S(1)}, u32[]{:S(2)}, u32[]{:S(2)}) collective-permute-start(bf16[144,512]{1,0:T(8,128)(2,1)S(1)} %fusion.33), channel_id=1, source_target_pairs={{0,8},{4,12},{8,0},{12,4},{1,9},{5,13},{9,1},{13,5},{2,10},{6,14},... | collective-permute-start | bytes 442376 | tf_op jit(solution)/shard_map/cond/branch_4_fun/ppermute | solution.py:549
  53.6 14.7 %collective-permute-start.37 = (bf16[144,1024]{1,0:T(8,128)(2,1)S(1)}, bf16[144,1024]{1,0:T(8,128)(2,1)S(1)}, u32[]{:S(2)}, u32[]{:S(2)}) collective-permute-start(bf16[144,1024]{1,0:T(8,128)(2,1)S(1)} %pad_maximum_fusion.4.refs_0_), channel_id=1, source_target_pairs={{0,8},{4,12},{8,0},{12,4},{1,9},{5,13},{9,1},{13,5},{2,10},{6,14},... | collective-permute-start | bytes 884744 | tf_op jit(solution)/shard_map/cond/branch_4_fun/ppermute | solution.py:549
  54.8 13.5 %collective-permute-start.39 = (bf16[144,1024]{1,0:T(8,128)(2,1)S(1)}, bf16[144,1024]{1,0:T(8,128)(2,1)S(1)}, u32[]{:S(2)}, u32[]{:S(2)}) collective-permute-start(bf16[144,1024]{1,0:T(8,128)(2,1)S(1)} %pad_maximum_fusion.4.refs_0_), channel_id=1, source_target_pairs={{0,4},{4,0},{8,12},{12,8},{1,5},{5,1},{9,13},{13,9},{2,6},{6,2},{1... | collective-permute-start | bytes 884744 | tf_op jit(solution)/shard_map/cond/branch_4_fun/ppermute | solution.py:549
  68.3 8.4 %collective-permute-start.38 = (bf16[144,1024]{1,0:T(8,128)(2,1)S(1)}, bf16[144,1024]{1,0:T(8,128)(2,1)S(1)}, u32[]{:S(2)}, u32[]{:S(2)}) collective-permute-start(bf16[144,1024]{1,0:T(8,128)(2,1)S(1)} %collective-permute-done.37.refs_0_), channel_id=1, source_target_pairs={{0,4},{4,0},{8,12},{12,8},{1,5},{5,1},{9,13},{13,9},{2,6},{6,2},{1... | collective-permute-start | bytes 884744 | tf_op jit(solution)/shard_map/cond/branch_4_fun/ppermute | solution.py:549
  79.7 1.8 %collective-permute-start.64 = (bf16[384,512]{1,0:T(8,128)(2,1)S(1)}, bf16[384,512]{1,0:T(8,128)(2,1)S(1)}, u32[]{:S(2)}, u32[]{:S(2)}) collective-permute-start(bf16[384,512]{1,0:T(8,128)(2,1)S(1)} %get-tuple-element.221), channel_id=1, source_target_pairs={{0,1},{1,0},{2,3},{3,2},{4,5},{5,4},{6,7},{7,6},{8,9},{9,8},{10,11... | collective-permute-start | bytes 1179656 | tf_op jit(solution)/shard_map/ppermute | solution.py:549
  81.5 4.9 %collective-permute-start.67 = (bf16[96,512]{1,0:T(8,128)(2,1)S(1)}, bf16[96,512]{1,0:T(8,128)(2,1)S(1)}, u32[]{:S(2)}, u32[]{:S(2)}) collective-permute-start(bf16[96,512]{1,0:T(8,128)(2,1)S(1)} %add_convert_fusion.1), channel_id=1, source_target_pairs={{0,2},{1,3},{2,0},{3,1},{4,6},{5,7},{6,4},{7,5},{8,10},{9,11},{10,... | collective-permute-start | bytes 294920 | tf_op jit(solution)/shard_map/ppermute | solution.py:549
  86.5 4.7 %collective-permute-start.65 = (bf16[96,512]{1,0:T(8,128)(2,1)S(1)}, bf16[96,512]{1,0:T(8,128)(2,1)S(1)}, u32[]{:S(2)}, u32[]{:S(2)}) collective-permute-start(bf16[96,512]{1,0:T(8,128)(2,1)S(1)} %get-tuple-element.237), channel_id=1, source_target_pairs={{0,2},{1,3},{2,0},{3,1},{4,6},{5,7},{6,4},{7,5},{8,10},{9,11},{10,... | collective-permute-start | bytes 294920 | tf_op jit(solution)/shard_map/ppermute | solution.py:549
  88.0 6.2 %collective-permute-start.69 = (bf16[48,512]{1,0:T(8,128)(2,1)S(1)}, bf16[48,512]{1,0:T(8,128)(2,1)S(1)}, u32[]{:S(2)}, u32[]{:S(2)}) collective-permute-start(bf16[48,512]{1,0:T(8,128)(2,1)S(1)} %get-tuple-element.238), channel_id=1, source_target_pairs={{0,12},{4,8},{8,4},{12,0},{1,13},{5,9},{9,5},{13,1},{2,14},{6,10},... | collective-permute-start | bytes 147464 | tf_op jit(solution)/shard_map/ppermute | solution.py:549
  90.1 5.5 %collective-permute-start.68 = (bf16[48,512]{1,0:T(8,128)(2,1)S(1)}, bf16[48,512]{1,0:T(8,128)(2,1)S(1)}, u32[]{:S(2)}, u32[]{:S(2)}) collective-permute-start(bf16[48,512]{1,0:T(8,128)(2,1)S(1)} %get-tuple-element.239), channel_id=1, source_target_pairs={{0,8},{4,12},{8,0},{12,4},{1,9},{5,13},{9,1},{13,5},{2,10},{6,14},... | collective-permute-start | bytes 147464 | tf_op jit(solution)/shard_map/ppermute | solution.py:549
  91.2 4.6 %collective-permute-start.66 = (bf16[48,512]{1,0:T(8,128)(2,1)S(1)}, bf16[48,512]{1,0:T(8,128)(2,1)S(1)}, u32[]{:S(2)}, u32[]{:S(2)}) collective-permute-start(bf16[48,512]{1,0:T(8,128)(2,1)S(1)} %get-tuple-element.240), channel_id=1, source_target_pairs={{0,4},{4,0},{8,12},{12,8},{1,5},{5,1},{9,13},{13,9},{2,6},{6,2},{1... | collective-permute-start | bytes 147464 | tf_op jit(solution)/shard_map/ppermute | solution.py:549
